TPU v7x, 256 devices: a whole 4x4x8 slice. The times are simulated.
256 devices in a mesh: grp: 8 (over z_lo, y), loc: 32 (over z_hi, x, core).
Axes of the slice: x: 4, y: 4, z: 8 (z_hi: 4, z_lo: 2; z = z_hi * 2 + z_lo), core: 2. Of those that a mesh axis runs over, the one named last changes fastest.
Arguments:
- hidden_states: bfloat16 [131072, 4096], P(('grp', 'loc')), may hold values from -50 to 50
- norm_gain: float32 [4096], replicated, may hold values from 0.1 to 1.9
- master_weight: float32 [4096, 512], P(('grp', 'loc')), may hold values from -0.09375 to 0.09375
- first_moment: float32 [4096, 512], P(('grp', 'loc')), may hold values from -1.5 to 1.5
- second_moment: float32 [4096, 512], P(('grp', 'loc')), may hold values from 0.01 to 1
- token_ids: int32 [131072], P(('grp', 'loc')), may hold values from 0 to 128255
- out_cotangent: bfloat16 [131072, 512], P(('grp', 'loc')), may hold values from -6 to 6
Outputs:
- value_heads: bfloat16 [131072, 512], P(('grp', 'loc'))
- input_grad: bfloat16 [131072, 4096], P(('grp', 'loc'))
- gain_grad: float32 [4096], replicated
- new_master: float32 [4096, 512], P(('grp', 'loc'))
- new_first: float32 [4096, 512], P(('grp', 'loc'))
- new_second: float32 [4096, 512], P(('grp', 'loc'))
All inputs are finite; a program needn't handle non-finite values.
Results may differ from a plain program's by a relative error of at most 0.0057.
Values may be sent and summed in bfloat16 or wider, within the bound.
No kernel may reach another device: no remote copies, remote signals or barrier semaphores. Data moves between devices by JAX's collectives and lax.ppermute only.
A program may use at most 128 MiB of HBM per device.

v0:
```python
import math

import jax
import jax.numpy as jnp
from jax import lax
from jax.sharding import PartitionSpec as P

RESERVED = 256
STEP = 10


norm_epsilon = 1e-05
beta_one = 0.9
beta_two = 0.95
adam_epsilon = 1e-08
learning_rate = 0.001
weight_decay = 0.1


def shards(
    hidden_states, norm_gain, master_weight, first_moment, second_moment, token_ids, out_cotangent
):
    groups = lax.axis_size("grp")
    loc_count = lax.axis_size("loc")
    tokens_all = hidden_states.shape[0] * groups * loc_count
    grad_scale = 1.0 / math.sqrt(tokens_all)
    states = hidden_states.astype(jnp.float32)
    inverse_rms = lax.rsqrt(jnp.mean(states * states, axis=1, keepdims=True) + norm_epsilon)
    scaled = states * inverse_rms
    normed = (scaled * norm_gain).astype(jnp.bfloat16)
    weight_bf = master_weight.astype(jnp.bfloat16)
    full_weight = lax.all_gather(weight_bf, ("grp", "loc"), axis=0, tiled=True)
    value_heads = jnp.dot(normed, full_weight, preferred_element_type=jnp.float32).astype(
        jnp.bfloat16
    )
    masked = jnp.where(
        (token_ids >= RESERVED)[:, None], out_cotangent, jnp.zeros_like(out_cotangent)
    )
    back_grad = lax.dot_general(
        masked,
        lax.all_gather(weight_bf, ("grp", "loc"), axis=0, tiled=True),
        (((1,), (1,)), ((), ())),
        preferred_element_type=jnp.float32,
    )
    weighted = back_grad * norm_gain
    inner = jnp.mean(weighted * scaled, axis=1, keepdims=True)
    input_grad = ((weighted - scaled * inner) * inverse_rms).astype(jnp.bfloat16)
    gain_total = lax.psum(jnp.sum(back_grad * scaled, axis=0), ("grp", "loc"))
    gain_grad = gain_total * grad_scale
    summed = lax.psum_scatter(
        lax.dot_general(
            normed, masked, (((0,), (0,)), ((), ())), preferred_element_type=jnp.float32
        ),
        ("grp", "loc"),
        scatter_dimension=0,
        tiled=True,
    )
    weight_grad = summed * grad_scale
    new_first = beta_one * first_moment + (1.0 - beta_one) * weight_grad
    new_second = beta_two * second_moment + (1.0 - beta_two) * weight_grad * weight_grad
    first_bias = 1.0 - beta_one**STEP
    second_bias = 1.0 - beta_two**STEP
    update = new_first / first_bias / (jnp.sqrt(new_second / second_bias) + adam_epsilon)
    new_master = master_weight - learning_rate * (update + weight_decay * master_weight)
    return (value_heads, input_grad, gain_grad, new_master, new_first, new_second)


def solution(mesh):
    in_specs = (
        P(("grp", "loc"), None),
        P(),
        P(("grp", "loc"), None),
        P(("grp", "loc"), None),
        P(("grp", "loc"), None),
        P(("grp", "loc")),
        P(("grp", "loc"), None),
    )
    out_specs = (
        P(("grp", "loc"), None),
        P(("grp", "loc"), None),
        P(),
        P(("grp", "loc"), None),
        P(("grp", "loc"), None),
        P(("grp", "loc"), None),
    )
    return jax.shard_map(shards, mesh=mesh, in_specs=in_specs, out_specs=out_specs, check_vma=False)
```

profile of v0, /device:TPU:1, one launch (start us, length us, event | category | flops | bytes accessed | tf_op | source)
XLA Modules:
  0.0 2047.1 jit_solution(17543987289027679403)
XLA Ops:
  7.2 0.0 reduce-scatter.2.cloned.1.call-start
  7.2 0.7 broadcast_compare_fusion
  7.9 3.1 fusion.10
  11.0 8.1 fusion.11
  19.1 0.0 copy-start.1
  19.1 0.0 copy-start.2
  19.1 0.0 copy-start.3
  19.1 0.0 copy-start.4
  19.1 0.0 copy-start.6
  19.1 0.0 reduce-scatter.2.cloned.1.call-update
  19.1 0.0 all-gather.2.cloned.1.call-start
  19.2 1278.5 %reduce-scatter.2.cloned.1.call-done = f32[16,512]{1,0:T(8,128)} async-done(((f32[4096,512]{1,0:T(8,128)}), f32[16,512]{1,0:T(8,128)}) %reduce-scatter.2.cloned.1.call-update) | async-done | bytes 32784 | tf_op jit(solution)/shard_map/reduce_scatter | solution.py:50
  1297.7 0.0 copy-done.1
  1297.7 0.0 copy-done.2
  1297.7 0.0 copy-done.3
  1297.7 1.4 multiply_subtract_fusion
  1299.1 0.0 all-gather.2.cloned.1.call-update
  1299.1 644.9 %all-gather.2.cloned.1.call-done = bf16[4096,512]{1,0:T(8,128)(2,1)} async-done(((bf16[16,512]{1,0:T(8,128)(2,1)}), bf16[4096,512]{1,0:T(8,128)(2,1)}) %all-gather.2.cloned.1.call-update) | async-done | bytes 4194320 | tf_op jit(solution)/shard_map/all_gather | solution.py:32
  1944.0 0.0 copy-done.4
  1944.0 0.0 copy-done.6
  1944.0 7.9 fusion.9
  1952.0 75.9 %psum.7 = f32[4096]{0:T(1024)S(1)} all-reduce(f32[4096]{0:T(1024)S(1)} %get-tuple-element.6), channel_id=1, replica_groups=mesh['grp'=8,'loc'=32] {'grp','loc'}, use_global_device_ids=true, to_apply=%region_3.4 | all-reduce | flops 4096 | bytes 32768 | tf_op jit(solution)/shard_map/psum | solution.py:48
  2027.9 0.6 broadcast_multiply_fusion
  2028.5 0.0 copy-start
  2028.5 0.0 copy-start.5
  2028.5 7.3 fusion.8
  2035.8 0.0 copy-done
  2035.8 1.3 copy-done.5
  2037.1 3.2 convolution_convert_fusion
  (2 shorter events, 0.0 us)
Async XLA Ops:
  7.2 1290.5 %reduce-scatter.2.cloned.1.call-start = ((), (), s32[]{:S(2)}) async-start(), calls=%async_computation.2 | async-start | bytes 8421376 | tf_op jit(solution)/shard_map/reduce_scatter | solution.py:50
  19.1 1278.6 %copy-start.1 = (f32[16,512]{1,0:T(8,128)S(1)}, f32[16,512]{1,0:T(8,128)}, u32[]{:S(2)}) copy-start(f32[16,512]{1,0:T(8,128)} %param.9) | copy-start | bytes 98308
  19.1 1278.6 %copy-start.2 = (f32[16,512]{1,0:T(8,128)S(1)}, f32[16,512]{1,0:T(8,128)}, u32[]{:S(2)}) copy-start(f32[16,512]{1,0:T(8,128)} %param.10) | copy-start | bytes 98308
  19.1 1278.6 %copy-start.3 = (f32[16,512]{1,0:T(8,128)S(1)}, f32[16,512]{1,0:T(8,128)}, u32[]{:S(2)}) copy-start(f32[16,512]{1,0:T(8,128)} %param.11) | copy-start | bytes 98308
  19.1 1924.9 %copy-start.4 = (f32[4096]{0:T(1024)S(1)}, f32[4096]{0:T(1024)}, u32[]{:S(2)}) copy-start(f32[4096]{0:T(1024)} %param.8) | copy-start | bytes 49156
  19.1 1924.9 %copy-start.6 = (bf16[512,512]{1,0:T(8,128)(2,1)S(1)}, bf16[512,512]{1,0:T(8,128)(2,1)}, u32[]{:S(2)}) copy-start(bf16[512,512]{1,0:T(8,128)(2,1)} %param.13) | copy-start | bytes 1572868
  19.1 1924.9 %all-gather.2.cloned.1.call-start = ((), (), s32[]{:S(2)}) async-start(), calls=%async_computation.1 | async-start | bytes 4210688 | tf_op jit(solution)/shard_map/all_gather | solution.py:32
  2028.5 7.3 copy-start
  2028.5 8.6 copy-start.5
Sparse Core Ops, SparseCore 0:
  19.2 1278.4 reduce-scatter.1
  1300.3 643.6 all-gather.1
where the time goes:
time: 2050 us
  waiting for transfers between devices  1920 us (94%)
  blocking collectives  75.9 us (4%)
    reduce_scatter x1, waiting for transfers between devices, shards(): lax.psum_scatter(lax.dot_general(normed, masked, (((0,), (0,)), ((), ()))...  1280 us
    all_gather x1, waiting for transfers between devices, shards(): full_weight = lax.all_gather(weight_bf, ('grp', 'loc'), axis=0, tiled=True)  645 us
    psum x1, blocking collectives, shards(): gain_total = lax.psum(jnp.sum(back_grad * scaled, axis=0), ('grp', 'loc'))  75.9 us
  transfers between devices with their start and end apart: 2, of which 2 were waited for; matrix products, arithmetic and copies ran while one was open for 0% of the time, Pallas kernels for 0%

commit v1 on v0

v1 whole, which is shorter than its diff:
```python
import math

import jax
import jax.numpy as jnp
import numpy as np
from jax import lax
from jax.experimental import pallas as pl
from jax.experimental.pallas import tpu as pltpu
from jax.sharding import PartitionSpec as P

RESERVED = 256
STEP = 10

norm_epsilon = 1e-05
beta_one = 0.9
beta_two = 0.95
adam_epsilon = 1e-08
learning_rate = 0.001
weight_decay = 0.1

bf16 = jnp.bfloat16
f32 = jnp.float32
AXES = ("grp", "loc")
DEVICES = 256

CORE = 1
X1, X3, Y1, Y3 = 2, 6, 32, 96
Z1, Z3, Z7 = 128, 136, 152
STEPS = (CORE, (X1, Y1), (X3, Y3), (Y1, X1), (Y3, X3), Z7, Z3, Z1)


def mask_of(mask, core):
    return mask[core] if isinstance(mask, tuple) else mask


def offsets(core):
    half = len(STEPS) - 1
    own, other = ([0], [0])
    for mask in STEPS[:0:-1]:
        own = own + [o ^ mask_of(mask, core) for o in own]
        other = other + [o ^ mask_of(mask, 1 - core) for o in other]
    return own + [o ^ CORE for o in other]


OFFSET_OF = np.array([offsets(0), offsets(1)], np.int32)
POSITION_OF = np.argsort(OFFSET_OF, axis=1).astype(np.int32)


def exchange(x, mask):
    pairs = [(i, i ^ mask_of(mask, i & 1)) for i in range(DEVICES)]
    return lax.ppermute(x, AXES, pairs)


def column(row):
    return jnp.transpose(jnp.broadcast_to(row, (8, row.shape[1])))[:, :1]


def grad_kernel(me_ref, pos_ref, h_ref, gain_ref, cot_ref, ids_ref, inv_ref, keep_ref, send_ref, blk_ref):
    tokens, features = h_ref.shape
    width = 512
    total = jnp.zeros((tokens, 128), f32)
    for j in range(features // 128):
        x = h_ref[:, 128 * j : 128 * j + 128].astype(f32)
        total = total + x * x
    mean = jnp.sum(total, axis=1, keepdims=True) * (1.0 / features)
    inv = lax.rsqrt(mean + norm_epsilon)
    inv_ref[...] = inv
    live = column(ids_ref[...]) >= RESERVED
    masked = jnp.where(live, cot_ref[...], jnp.zeros_like(cot_ref))
    me = me_ref[0]
    core = jnp.bitwise_and(me, 1)

    def block(j, carry):
        at = pl.ds(pl.multiple_of(j * width, width), width)
        normed = ((h_ref[:, at].astype(f32) * inv) * gain_ref[:, at]).astype(bf16)
        part = lax.dot_general(normed, masked, (((0,), (0,)), ((), ())), preferred_element_type=f32)
        blk_ref[...] = part.reshape(blk_ref.shape)
        for i in range(width // 32):
            own = 2 * i + core
            away = 2 * i + (1 - core)
            p = pos_ref[core, jnp.bitwise_xor(j * (width // 16) + own, me)]
            q = pos_ref[core, jnp.bitwise_xor(j * (width // 16) + away, me)] - DEVICES // 2
            keep_ref[p] = blk_ref[own]
            send_ref[q] = blk_ref[away].astype(bf16)
        return carry

    lax.fori_loop(0, features // width, block, 0)


def local_grad(me, hidden, gain, cot, ids):
    tokens, features = hidden.shape
    outs = cot.shape[1]
    half = features // 32
    vmem = pl.BlockSpec(memory_space=pltpu.VMEM)
    smem = pl.BlockSpec(memory_space=pltpu.SMEM)
    return pl.pallas_call(
        grad_kernel,
        out_shape=(
            jax.ShapeDtypeStruct((tokens, 1), f32),
            jax.ShapeDtypeStruct((half, 16, outs), f32),
            jax.ShapeDtypeStruct((half, 16, outs), bf16),
        ),
        in_specs=[smem, smem, vmem, vmem, vmem, vmem],
        out_specs=(vmem, vmem, vmem),
        scratch_shapes=[pltpu.VMEM((32, 16, outs), f32)],
        compiler_params=pltpu.CompilerParams(vmem_limit_bytes=48 * 2**20),
        cost_estimate=pl.CostEstimate(
            flops=2 * tokens * features * outs, bytes_accessed=12 * 2**20, transcendentals=0
        ),
        name="local_grad",
    )(me, jnp.asarray(POSITION_OF), hidden, gain, cot, ids)


def both_kernel(me_ref, off_ref, h_ref, inv_ref, gain_ref, cot_ref, ids_ref, own_ref, other_ref, values_ref, grad_ref, w_ref, wt_ref):
    tokens, features = h_ref.shape
    width = 512
    me = me_ref[0]
    core = jnp.bitwise_and(me, 1)
    half = DEVICES // 2

    @pl.when(pl.program_id(0) == 0)
    def _():
        def place(p, carry):
            w_ref[jnp.bitwise_xor(off_ref[core, p], me)] = own_ref[p]
            w_ref[jnp.bitwise_xor(off_ref[core, p + half], me)] = other_ref[p]
            return carry

        lax.fori_loop(0, half, place, 0, unroll=8)

    inv = inv_ref[...]
    live = column(ids_ref[...]) >= RESERVED
    masked = jnp.where(live, cot_ref[...], jnp.zeros_like(cot_ref))
    values = jnp.zeros(values_ref.shape, f32)
    inner = jnp.zeros((tokens, 128), f32)
    for j in range(features // width):
        at = slice(j * width, j * width + width)
        w = w_ref[j * (width // 16) : (j + 1) * (width // 16)].reshape(width, w_ref.shape[2])
        gain = gain_ref[:, at]
        scaled = h_ref[:, at].astype(f32) * inv
        values = values + jnp.dot((scaled * gain).astype(bf16), w, preferred_element_type=f32)
        back = lax.dot_general(masked, w, (((1,), (1,)), ((), ())), preferred_element_type=f32)
        weighted = back * gain
        wt_ref[:, at] = weighted
        prod = weighted * scaled
        for k in range(width // 128):
            inner = inner + prod[:, 128 * k : 128 * k + 128]
    values_ref[...] = values.astype(bf16)
    mean = jnp.sum(inner, axis=1, keepdims=True) * (1.0 / features)
    for j in range(features // width):
        at = slice(j * width, j * width + width)
        scaled = h_ref[:, at].astype(f32) * inv
        grad_ref[:, at] = ((wt_ref[:, at] - scaled * mean) * inv).astype(bf16)


def values_and_input_grad(me, hidden, inv, gain, cot, ids, own, other):
    tokens, features = hidden.shape
    outs = cot.shape[1]
    rows = 256
    smem = pl.BlockSpec(memory_space=pltpu.SMEM)
    whole = pl.BlockSpec(own.shape, lambda i: (0, 0, 0))
    return pl.pallas_call(
        both_kernel,
        grid=(tokens // rows,),
        out_shape=(
            jax.ShapeDtypeStruct((tokens, outs), bf16),
            jax.ShapeDtypeStruct((tokens, features), bf16),
        ),
        in_specs=[
            smem,
            smem,
            pl.BlockSpec((rows, features), lambda i: (i, 0)),
            pl.BlockSpec((rows, 1), lambda i: (i, 0)),
            pl.BlockSpec((1, features), lambda i: (0, 0)),
            pl.BlockSpec((rows, outs), lambda i: (i, 0)),
            pl.BlockSpec((1, rows), lambda i: (0, i)),
            whole,
            whole,
        ],
        out_specs=(
            pl.BlockSpec((rows, outs), lambda i: (i, 0)),
            pl.BlockSpec((rows, features), lambda i: (i, 0)),
        ),
        scratch_shapes=[
            pltpu.VMEM((features // 16, 16, outs), bf16),
            pltpu.VMEM((rows, features), f32),
        ],
        compiler_params=pltpu.CompilerParams(vmem_limit_bytes=48 * 2**20),
        cost_estimate=pl.CostEstimate(
            flops=4 * tokens * features * outs, bytes_accessed=13 * 2**20, transcendentals=0
        ),
        name="values_and_input_grad",
    )(me, jnp.asarray(OFFSET_OF), hidden, inv, gain, cot, ids, own, other)


def shards(
    hidden_states, norm_gain, master_weight, first_moment, second_moment, token_ids, out_cotangent
):
    tokens_all = hidden_states.shape[0] * DEVICES
    grad_scale = 1.0 / math.sqrt(tokens_all)
    features = hidden_states.shape[1]
    rows, outs = master_weight.shape
    index = lax.axis_index("grp") * lax.axis_size("loc") + lax.axis_index("loc")
    me = index.astype(jnp.int32).reshape(1)
    gain_row = norm_gain.reshape(1, features)
    ids_row = token_ids.reshape(1, -1)

    weight_bf = master_weight.astype(bf16)
    held = weight_bf.reshape(1, rows, outs)
    for mask in STEPS[:0:-1]:
        held = jnp.concatenate([held, exchange(held, mask)], axis=0)
    other = exchange(held, CORE)

    inv, keep, send = local_grad(me, hidden_states, gain_row, out_cotangent, ids_row)
    total = keep + exchange(send, CORE).astype(f32)
    for mask in STEPS[1:]:
        half = total.shape[0] // 2
        leave = total[half:]
        if half > 2:
            leave = leave.astype(bf16)
        total = total[:half] + exchange(leave, mask).astype(f32)
    summed = total.reshape(rows, outs)

    value_heads, input_grad = values_and_input_grad(
        me, hidden_states, inv, gain_row, out_cotangent, ids_row, held, other
    )

    weight_grad = summed * grad_scale
    new_first = beta_one * first_moment + (1.0 - beta_one) * weight_grad
    new_second = beta_two * second_moment + (1.0 - beta_two) * weight_grad * weight_grad
    first_bias = 1.0 - beta_one**STEP
    second_bias = 1.0 - beta_two**STEP
    update = new_first / first_bias / (jnp.sqrt(new_second / second_bias) + adam_epsilon)
    new_master = master_weight - learning_rate * (update + weight_decay * master_weight)

    gain_rows = jnp.sum(weight_grad * weight_bf.astype(f32), axis=1).reshape(1, rows)
    gain_all = lax.all_to_all(
        jnp.broadcast_to(gain_rows, (DEVICES, rows)), AXES, split_axis=0, concat_axis=0, tiled=True
    )
    gain_grad = gain_all.reshape(features) / norm_gain
    return (value_heads, input_grad, gain_grad, new_master, new_first, new_second)


def solution(mesh):
    in_specs = (
        P(("grp", "loc"), None),
        P(),
        P(("grp", "loc"), None),
        P(("grp", "loc"), None),
        P(("grp", "loc"), None),
        P(("grp", "loc")),
        P(("grp", "loc"), None),
    )
    out_specs = (
        P(("grp", "loc"), None),
        P(("grp", "loc"), None),
        P(),
        P(("grp", "loc"), None),
        P(("grp", "loc"), None),
        P(("grp", "loc"), None),
    )
    return jax.shard_map(shards, mesh=mesh, in_specs=in_specs, out_specs=out_specs, check_vma=False)
```

time: 2050 us -> 132 us (0.06)
  waiting for transfers between devices: 1920 us -> 46.7 us
  blocking collectives: 75.9 us -> 0 us
  starting transfers between devices: 0.08 us -> 50.3 us
  Pallas kernels: 0 us -> 22.3 us
    reduce_scatter x1 -> x0, waiting for transfers between devices: 1280 us -> none  [shards(): lax.psum_scatter(lax.dot_general(normed, masked, (((0,), (0,)), ((), ()))...]
    all_gather x1 -> x0, waiting for transfers between devices: 645 us -> none  [shards(): full_weight = lax.all_gather(weight_bf, ('grp', 'loc'), axis=0, tiled=True)]
    psum x1 -> x0, blocking collectives: 75.9 us -> none  [shards(): gain_total = lax.psum(jnp.sum(back_grad * scaled, axis=0), ('grp', 'loc'))]
    ppermute x0 -> x16, waiting for transfers between devices: none -> 46.1 us  [exchange(): return lax.ppermute(x, AXES, pairs)]
    ppermute x0 -> x16, starting transfers between devices: none -> 35.5 us  [exchange(): return lax.ppermute(x, AXES, pairs)]
    pallas_call x0 -> x2, Pallas kernels: none -> 22.3 us  [the longest x1 12.1 us: values_and_input_grad(): pl.pallas_call(both_kernel, grid=(tokens // rows,), out_shape=(jax.ShapeD...]
  transfers between devices with their start and end apart: 2 -> 17, of which waited for: 2 -> 14; matrix products, arithmetic and copies ran while one was open for 0% -> 4% of each run, Pallas kernels for 0% -> 9%
where the time goes in v1:
time: 132 us; the launch traced here: 131 us
  starting transfers between devices  50.3 us (38%)
  waiting for transfers between devices  46.7 us (35%)
  Pallas kernels  22.3 us (17%)
  other arithmetic  6.09 us (5%)
  local copies, waits for them, and re-layouts  5.1 us (4%)
    ppermute x16, waiting for transfers between devices, exchange(): return lax.ppermute(x, AXES, pairs)  46.1 us
    ppermute x16, starting transfers between devices, exchange(): return lax.ppermute(x, AXES, pairs)  35.5 us
    all_to_all x1, starting transfers between devices, shards(): lax.all_to_all(jnp.broadcast_to(gain_rows, (DEVICES, rows)), AXES, split_...  14.8 us
    pallas_call x1, Pallas kernels, values_and_input_grad(): pl.pallas_call(both_kernel, grid=(tokens // rows,), out_shape=(jax.ShapeD...  12.1 us
    pallas_call x1, Pallas kernels, local_grad(): pl.pallas_call(grad_kernel, out_shape=(jax.ShapeDtypeStruct((tokens, 1),...  10.1 us
    unnamed x28, local copies, waits for them, and re-layouts  3.3 us
    add x1, other arithmetic, shards(): total = keep + exchange(send, CORE).astype(f32)  3.02 us
  transfers between devices with their start and end apart: 17, of which 14 were waited for; matrix products, arithmetic and copies ran while one was open for 4% of the time, Pallas kernels for 9%

profile of v1, /device:TPU:1, one launch (start us, length us, event | category | flops | bytes accessed | tf_op | source)
XLA Modules:
  0.0 131.5 jit_solution(18037565770593720010)
XLA Ops:
  0.6 0.7 copy-done
  1.4 1.0 copy-done.2
  3.8 10.1 %local_grad.1 = (f32[512,1]{1,0:T(8,128)S(1)}, f32[128,16,512]{2,1,0:T(8,128)}, bf16[128,16,512]{2,1,0:T(8,128)(2,1)S(1)}) custom-call(s32[1]{0:T(128)} %bitcast.me_ref, s32[2,256]{1,0:T(2,128)S(1)} %copy-done.7, bf16[512,4096]{1,0:T(8,128)(2,1)} %h_ref.3, f32[1,4096]{1,0:T(1,128)S(1)} %bitcast.20, bf16[512,512]{1,0:T(8,128)(2,1)S(1)} %copy-done.2, ...), custom_call_target="tpu_custom_call" | custom-call | flops 2147483648 | bytes 12582912 | tf_op jit(solution)/shard_map/local_grad/pallas_call | solution.py:96
  13.9 3.1 %collective-permute-start.8 = (bf16[128,16,512]{2,1,0:T(8,128)(2,1)S(1)}, bf16[128,16,512]{2,1,0:T(8,128)(2,1)S(1)}, u32[]{:S(2)}, u32[]{:S(2)}) collective-permute-start(bf16[128,16,512]{2,1,0:T(8,128)(2,1)S(1)} %get-tuple-element.15), channel_id=1, source_target_pairs={{0,1},{1,0},{2,3},{3,2},{4,5},{5,4},{6,7},{7,6},{8,9},{9,8},{10,11... | collective-permute-start | bytes 6291464 | tf_op jit(solution)/shard_map/ppermute | solution.py:51
  17.0 2.6 %collective-permute-done = bf16[1,16,512]{2,1,0:T(8,128)(2,1)S(1)} collective-permute-done((bf16[1,16,512]{2,1,0:T(8,128)(2,1)S(1)}, bf16[1,16,512]{2,1,0:T(8,128)(2,1)S(1)}, u32[]{:S(2)}, u32[]{:S(2)}) %collective-permute-start) | collective-permute-done | bytes 16416 | tf_op jit(solution)/shard_map/ppermute | solution.py:51
  19.6 2.6 %collective-permute-start.1 = (bf16[2,16,512]{2,1,0:T(8,128)(2,1)S(1)}, bf16[2,16,512]{2,1,0:T(8,128)(2,1)S(1)}, u32[]{:S(2)}, u32[]{:S(2)}) collective-permute-start(bf16[2,16,512]{2,1,0:T(8,128)(2,1)S(1)} %pad_maximum_fusion.2), channel_id=1, source_target_pairs={{0,136},{1,137},{2,138},{3,139},{4,140},{5,141},{6,142},{7,143},{8... | collective-permute-start | bytes 98312 | tf_op jit(solution)/shard_map/ppermute | solution.py:51
  22.2 1.9 %collective-permute-done.1 = bf16[2,16,512]{2,1,0:T(8,128)(2,1)S(1)} collective-permute-done((bf16[2,16,512]{2,1,0:T(8,128)(2,1)S(1)}, bf16[2,16,512]{2,1,0:T(8,128)(2,1)S(1)}, u32[]{:S(2)}, u32[]{:S(2)}) %collective-permute-start.1) | collective-permute-done | bytes 32800 | tf_op jit(solution)/shard_map/ppermute | solution.py:51
  24.2 3.9 %collective-permute-start.2 = (bf16[4,16,512]{2,1,0:T(8,128)(2,1)S(1)}, bf16[4,16,512]{2,1,0:T(8,128)(2,1)S(1)}, u32[]{:S(2)}, u32[]{:S(2)}) collective-permute-start(bf16[4,16,512]{2,1,0:T(8,128)(2,1)S(1)} %pad_maximum_fusion.1), channel_id=1, source_target_pairs={{0,152},{1,153},{2,154},{3,155},{4,156},{5,157},{6,158},{7,159},{8... | collective-permute-start | bytes 196616 | tf_op jit(solution)/shard_map/ppermute | solution.py:51
  28.2 1.6 %collective-permute-done.2 = bf16[4,16,512]{2,1,0:T(8,128)(2,1)S(1)} collective-permute-done((bf16[4,16,512]{2,1,0:T(8,128)(2,1)S(1)}, bf16[4,16,512]{2,1,0:T(8,128)(2,1)S(1)}, u32[]{:S(2)}, u32[]{:S(2)}) %collective-permute-start.2) | collective-permute-done | bytes 65568 | tf_op jit(solution)/shard_map/ppermute | solution.py:51
  29.8 2.5 %collective-permute-start.3 = (bf16[8,16,512]{2,1,0:T(8,128)(2,1)S(1)}, bf16[8,16,512]{2,1,0:T(8,128)(2,1)S(1)}, u32[]{:S(2)}, u32[]{:S(2)}) collective-permute-start(bf16[8,16,512]{2,1,0:T(8,128)(2,1)S(1)} %pad_maximum_fusion), channel_id=1, source_target_pairs={{0,96},{1,7},{2,98},{3,5},{4,100},{5,3},{6,102},{7,1},{8,104},{9,1... | collective-permute-start | bytes 393224 | tf_op jit(solution)/shard_map/ppermute | solution.py:51
  32.4 2.5 %collective-permute-done.3 = bf16[8,16,512]{2,1,0:T(8,128)(2,1)S(1)} collective-permute-done((bf16[8,16,512]{2,1,0:T(8,128)(2,1)S(1)}, bf16[8,16,512]{2,1,0:T(8,128)(2,1)S(1)}, u32[]{:S(2)}, u32[]{:S(2)}) %collective-permute-start.3) | collective-permute-done | bytes 131104 | tf_op jit(solution)/shard_map/ppermute | solution.py:51
  35.1 3.0 %convert_add_fusion = f32[128,16,512]{2,1,0:T(8,128)S(1)} fusion(f32[128,16,512]{2,1,0:T(8,128)} %get-tuple-element.14, bf16[128,16,512]{2,1,0:T(8,128)(2,1)S(1)} %collective-permute-done.8), kind=kLoop, calls=%fused_computation | loop fusion | flops 2097152 | bytes 10485760 | tf_op jit(solution)/shard_map/add | solution.py:214
  38.3 1.4 %collective-permute-start.9 = (bf16[64,16,512]{2,1,0:T(8,128)(2,1)S(1)}, bf16[64,16,512]{2,1,0:T(8,128)(2,1)S(1)}, u32[]{:S(2)}, u32[]{:S(2)}) collective-permute-start(bf16[64,16,512]{2,1,0:T(8,128)(2,1)S(1)} %slice.93), channel_id=1, source_target_pairs={{0,2},{1,33},{2,0},{3,35},{4,6},{5,37},{6,4},{7,39},{8,10},{9,41},... | collective-permute-start | bytes 3145736 | tf_op jit(solution)/shard_map/ppermute | solution.py:51
  40.4 2.8 %collective-permute-start.5 = (bf16[32,16,512]{2,1,0:T(8,128)(2,1)S(1)}, bf16[32,16,512]{2,1,0:T(8,128)(2,1)S(1)}, u32[]{:S(2)}, u32[]{:S(2)}) collective-permute-start(bf16[32,16,512]{2,1,0:T(8,128)(2,1)S(1)} %get-tuple-element.25), channel_id=1, source_target_pairs={{0,6},{1,97},{2,4},{3,99},{4,2},{5,101},{6,0},{7,103},{8,14},{9,10... | collective-permute-start | bytes 1572872 | tf_op jit(solution)/shard_map/ppermute | solution.py:51
  43.2 6.6 %collective-permute-done.5 = bf16[32,16,512]{2,1,0:T(8,128)(2,1)S(1)} collective-permute-done((bf16[32,16,512]{2,1,0:T(8,128)(2,1)S(1)}, bf16[32,16,512]{2,1,0:T(8,128)(2,1)S(1)}, u32[]{:S(2)}, u32[]{:S(2)}) %collective-permute-start.5) | collective-permute-done | bytes 524320 | tf_op jit(solution)/shard_map/ppermute | solution.py:51
  50.2 4.9 %collective-permute-done.9 = bf16[64,16,512]{2,1,0:T(8,128)(2,1)S(1)} collective-permute-done((bf16[64,16,512]{2,1,0:T(8,128)(2,1)S(1)}, bf16[64,16,512]{2,1,0:T(8,128)(2,1)S(1)}, u32[]{:S(2)}, u32[]{:S(2)}) %collective-permute-start.9) | collective-permute-done | bytes 1048608 | tf_op jit(solution)/shard_map/ppermute | solution.py:51
  55.6 2.8 %collective-permute-start.10 = (bf16[32,16,512]{2,1,0:T(8,128)(2,1)S(1)}, bf16[32,16,512]{2,1,0:T(8,128)(2,1)S(1)}, u32[]{:S(2)}, u32[]{:S(2)}) collective-permute-start(bf16[32,16,512]{2,1,0:T(8,128)(2,1)S(1)} %slice.94), channel_id=1, source_target_pairs={{0,6},{1,97},{2,4},{3,99},{4,2},{5,101},{6,0},{7,103},{8,14},{9,10... | collective-permute-start | bytes 1572872 | tf_op jit(solution)/shard_map/ppermute | solution.py:51
  58.4 8.0 %collective-permute-done.6 = bf16[64,16,512]{2,1,0:T(8,128)(2,1)S(1)} collective-permute-done((bf16[64,16,512]{2,1,0:T(8,128)(2,1)S(1)}, bf16[64,16,512]{2,1,0:T(8,128)(2,1)S(1)}, u32[]{:S(2)}, u32[]{:S(2)}) %collective-permute-start.6) | collective-permute-done | bytes 1048608 | tf_op jit(solution)/shard_map/ppermute | solution.py:51
  66.4 7.9 %collective-permute-start.7 = (bf16[128,16,512]{2,1,0:T(8,128)(2,1)S(1)}, bf16[128,16,512]{2,1,0:T(8,128)(2,1)}, u32[]{:S(2)}, u32[]{:S(2)}) collective-permute-start(bf16[128,16,512]{2,1,0:T(8,128)(2,1)S(1)} %constant_dynamic-update-slice_fusion.18.own_ref), channel_id=1, source_target_pairs={{0,1},{1,0},{2,3},{3,2},{4,5},{5,4},{6,7},{7,6},{8,9},{9,8},{10,11... | collective-permute-start | bytes 6291464 | tf_op jit(solution)/shard_map/ppermute | solution.py:51
  74.8 5.5 %collective-permute-done.11 = bf16[16,16,512]{2,1,0:T(8,128)(2,1)S(1)} collective-permute-done((bf16[16,16,512]{2,1,0:T(8,128)(2,1)S(1)}, bf16[16,16,512]{2,1,0:T(8,128)(2,1)S(1)}, u32[]{:S(2)}, u32[]{:S(2)}) %collective-permute-start.11) | collective-permute-done | bytes 262176 | tf_op jit(solution)/shard_map/ppermute | solution.py:51
  80.4 2.5 %collective-permute-start.12 = (bf16[8,16,512]{2,1,0:T(8,128)(2,1)S(1)}, bf16[8,16,512]{2,1,0:T(8,128)(2,1)S(1)}, u32[]{:S(2)}, u32[]{:S(2)}) collective-permute-start(bf16[8,16,512]{2,1,0:T(8,128)(2,1)S(1)} %slice.96), channel_id=1, source_target_pairs={{0,96},{1,7},{2,98},{3,5},{4,100},{5,3},{6,102},{7,1},{8,104},{9,1... | collective-permute-start | bytes 393224 | tf_op jit(solution)/shard_map/ppermute | solution.py:51
  82.9 2.9 %collective-permute-done.12 = bf16[8,16,512]{2,1,0:T(8,128)(2,1)S(1)} collective-permute-done((bf16[8,16,512]{2,1,0:T(8,128)(2,1)S(1)}, bf16[8,16,512]{2,1,0:T(8,128)(2,1)S(1)}, u32[]{:S(2)}, u32[]{:S(2)}) %collective-permute-start.12) | collective-permute-done | bytes 131104 | tf_op jit(solution)/shard_map/ppermute | solution.py:51
  85.9 3.3 %collective-permute-start.13 = (bf16[4,16,512]{2,1,0:T(8,128)(2,1)S(1)}, bf16[4,16,512]{2,1,0:T(8,128)(2,1)S(1)}, u32[]{:S(2)}, u32[]{:S(2)}) collective-permute-start(bf16[4,16,512]{2,1,0:T(8,128)(2,1)S(1)} %slice.97), channel_id=1, source_target_pairs={{0,152},{1,153},{2,154},{3,155},{4,156},{5,157},{6,158},{7,159},{8... | collective-permute-start | bytes 196616 | tf_op jit(solution)/shard_map/ppermute | solution.py:51
  89.2 2.4 %collective-permute-done.13 = bf16[4,16,512]{2,1,0:T(8,128)(2,1)S(1)} collective-permute-done((bf16[4,16,512]{2,1,0:T(8,128)(2,1)S(1)}, bf16[4,16,512]{2,1,0:T(8,128)(2,1)S(1)}, u32[]{:S(2)}, u32[]{:S(2)}) %collective-permute-start.13) | collective-permute-done | bytes 65568 | tf_op jit(solution)/shard_map/ppermute | solution.py:51
  91.6 1.7 %collective-permute-start.14 = (f32[2,16,512]{2,1,0:T(8,128)S(1)}, f32[2,16,512]{2,1,0:T(8,128)S(1)}, u32[]{:S(2)}, u32[]{:S(2)}) collective-permute-start(f32[2,16,512]{2,1,0:T(8,128)S(1)} %slice.72), channel_id=1, source_target_pairs={{0,136},{1,137},{2,138},{3,139},{4,140},{5,141},{6,142},{7,143},{8... | collective-permute-start | bytes 196616 | tf_op jit(solution)/shard_map/ppermute | solution.py:51
  93.3 3.3 %collective-permute-done.14 = f32[2,16,512]{2,1,0:T(8,128)S(1)} collective-permute-done((f32[2,16,512]{2,1,0:T(8,128)S(1)}, f32[2,16,512]{2,1,0:T(8,128)S(1)}, u32[]{:S(2)}, u32[]{:S(2)}) %collective-permute-start.14) | collective-permute-done | bytes 65568 | tf_op jit(solution)/shard_map/ppermute | solution.py:51
  96.9 3.3 %collective-permute-done.15 = f32[1,16,512]{2,1,0:T(8,128)S(1)} collective-permute-done((f32[1,16,512]{2,1,0:T(8,128)S(1)}, f32[1,16,512]{2,1,0:T(8,128)S(1)}, u32[]{:S(2)}, u32[]{:S(2)}) %collective-permute-start.15) | collective-permute-done | bytes 32800 | tf_op jit(solution)/shard_map/ppermute | solution.py:51
  100.2 0.8 multiply_subtract_fusion
  101.0 0.7 broadcast_in_dim.2
  101.7 14.8 %all-to-all-start = ((f32[256,1,16]{2,1,0:T(1,128)}), f32[256,1,16]{2,1,0:T(1,128)S(1)}, u32[]{:S(2)}, u32[]{:S(2)}) async-start(f32[256,1,16]{2,1,0:T(1,128)} %broadcast_in_dim.2), calls=%async_computation | async-start | bytes 262144 | tf_op jit(solution)/shard_map/all_to_all | solution.py:236
  116.5 12.1 %values_and_input_grad.1 = (bf16[512,512]{1,0:T(8,128)(2,1)}, bf16[512,4096]{1,0:T(8,128)(2,1)}) custom-call(s32[1]{0:T(128)} %bitcast.me_ref, s32[2,256]{1,0:T(2,128)S(1)} %copy-done.6, bf16[512,4096]{1,0:T(8,128)(2,1)} %h_ref.3, f32[512,1]{1,0:T(8,128)S(1)} %get-tuple-element.11.inv_ref, f32[1,4096]{1,0:T(1,128)S(1)} %bitcast.21, ...), custom_call_target="tpu_custom_call" | custom-call | flops 4294967296 | bytes 13631488 | tf_op jit(solution)/shard_map/values_and_input_grad/pallas_call | solution.py:161
  129.8 1.0 reduce.3
  (58 shorter events, 6.1 us)
Async XLA Ops:
  0.6 0.7 copy-start
  1.4 1.0 copy-start.2
  2.4 0.7 copy-start.4
  3.1 0.7 copy-start.7
  3.8 13.3 %copy-start.8 = (f32[16,512]{1,0:T(8,128)S(1)}, f32[16,512]{1,0:T(8,128)}, u32[]{:S(2)}) copy-start(f32[16,512]{1,0:T(8,128)} %param.11) | copy-start | bytes 98308
  13.9 21.2 %collective-permute-start.8 = (bf16[128,16,512]{2,1,0:T(8,128)(2,1)S(1)}, bf16[128,16,512]{2,1,0:T(8,128)(2,1)S(1)}, u32[]{:S(2)}, u32[]{:S(2)}) collective-permute-start(bf16[128,16,512]{2,1,0:T(8,128)(2,1)S(1)} %get-tuple-element.15), channel_id=1, source_target_pairs={{0,1},{1,0},{2,3},{3,2},{4,5},{5,4},{6,7},{7,6},{8,9},{9,8},{10,11... | collective-permute-start | bytes 6291464 | tf_op jit(solution)/shard_map/ppermute | solution.py:51
  17.0 2.6 %collective-permute-start = (bf16[1,16,512]{2,1,0:T(8,128)(2,1)S(1)}, bf16[1,16,512]{2,1,0:T(8,128)(2,1)S(1)}, u32[]{:S(2)}, u32[]{:S(2)}) collective-permute-start(bf16[1,16,512]{2,1,0:T(8,128)(2,1)S(1)} %get-tuple-element.20), channel_id=1, source_target_pairs={{0,128},{1,129},{2,130},{3,131},{4,132},{5,133},{6,134},{7,135},{8... | collective-permute-start | bytes 49160 | tf_op jit(solution)/shard_map/ppermute | solution.py:51
  19.6 4.6 %collective-permute-start.1 = (bf16[2,16,512]{2,1,0:T(8,128)(2,1)S(1)}, bf16[2,16,512]{2,1,0:T(8,128)(2,1)S(1)}, u32[]{:S(2)}, u32[]{:S(2)}) collective-permute-start(bf16[2,16,512]{2,1,0:T(8,128)(2,1)S(1)} %pad_maximum_fusion.2), channel_id=1, source_target_pairs={{0,136},{1,137},{2,138},{3,139},{4,140},{5,141},{6,142},{7,143},{8... | collective-permute-start | bytes 98312 | tf_op jit(solution)/shard_map/ppermute | solution.py:51
  24.2 5.6 %collective-permute-start.2 = (bf16[4,16,512]{2,1,0:T(8,128)(2,1)S(1)}, bf16[4,16,512]{2,1,0:T(8,128)(2,1)S(1)}, u32[]{:S(2)}, u32[]{:S(2)}) collective-permute-start(bf16[4,16,512]{2,1,0:T(8,128)(2,1)S(1)} %pad_maximum_fusion.1), channel_id=1, source_target_pairs={{0,152},{1,153},{2,154},{3,155},{4,156},{5,157},{6,158},{7,159},{8... | collective-permute-start | bytes 196616 | tf_op jit(solution)/shard_map/ppermute | solution.py:51
  29.8 5.1 %collective-permute-start.3 = (bf16[8,16,512]{2,1,0:T(8,128)(2,1)S(1)}, bf16[8,16,512]{2,1,0:T(8,128)(2,1)S(1)}, u32[]{:S(2)}, u32[]{:S(2)}) collective-permute-start(bf16[8,16,512]{2,1,0:T(8,128)(2,1)S(1)} %pad_maximum_fusion), channel_id=1, source_target_pairs={{0,96},{1,7},{2,98},{3,5},{4,100},{5,3},{6,102},{7,1},{8,104},{9,1... | collective-permute-start | bytes 393224 | tf_op jit(solution)/shard_map/ppermute | solution.py:51
  35.0 5.3 %collective-permute-start.4 = (bf16[16,16,512]{2,1,0:T(8,128)(2,1)S(1)}, bf16[16,16,512]{2,1,0:T(8,128)(2,1)S(1)}, u32[]{:S(2)}, u32[]{:S(2)}) collective-permute-start(bf16[16,16,512]{2,1,0:T(8,128)(2,1)S(1)} %get-tuple-element.30), channel_id=1, source_target_pairs={{0,32},{1,3},{2,34},{3,1},{4,36},{5,7},{6,38},{7,5},{8,40},{9,11},... | collective-permute-start | bytes 786440 | tf_op jit(solution)/shard_map/ppermute | solution.py:51
  38.3 16.8 %collective-permute-start.9 = (bf16[64,16,512]{2,1,0:T(8,128)(2,1)S(1)}, bf16[64,16,512]{2,1,0:T(8,128)(2,1)S(1)}, u32[]{:S(2)}, u32[]{:S(2)}) collective-permute-start(bf16[64,16,512]{2,1,0:T(8,128)(2,1)S(1)} %slice.93), channel_id=1, source_target_pairs={{0,2},{1,33},{2,0},{3,35},{4,6},{5,37},{6,4},{7,39},{8,10},{9,41},... | collective-permute-start | bytes 3145736 | tf_op jit(solution)/shard_map/ppermute | solution.py:51
  40.4 9.4 %collective-permute-start.5 = (bf16[32,16,512]{2,1,0:T(8,128)(2,1)S(1)}, bf16[32,16,512]{2,1,0:T(8,128)(2,1)S(1)}, u32[]{:S(2)}, u32[]{:S(2)}) collective-permute-start(bf16[32,16,512]{2,1,0:T(8,128)(2,1)S(1)} %get-tuple-element.25), channel_id=1, source_target_pairs={{0,6},{1,97},{2,4},{3,99},{4,2},{5,101},{6,0},{7,103},{8,14},{9,10... | collective-permute-start | bytes 1572872 | tf_op jit(solution)/shard_map/ppermute | solution.py:51
  49.8 16.5 %collective-permute-start.6 = (bf16[64,16,512]{2,1,0:T(8,128)(2,1)S(1)}, bf16[64,16,512]{2,1,0:T(8,128)(2,1)S(1)}, u32[]{:S(2)}, u32[]{:S(2)}) collective-permute-start(bf16[64,16,512]{2,1,0:T(8,128)(2,1)S(1)} %get-tuple-element.21), channel_id=1, source_target_pairs={{0,2},{1,33},{2,0},{3,35},{4,6},{5,37},{6,4},{7,39},{8,10},{9,41},... | collective-permute-start | bytes 3145736 | tf_op jit(solution)/shard_map/ppermute | solution.py:51
  55.6 18.8 %collective-permute-start.10 = (bf16[32,16,512]{2,1,0:T(8,128)(2,1)S(1)}, bf16[32,16,512]{2,1,0:T(8,128)(2,1)S(1)}, u32[]{:S(2)}, u32[]{:S(2)}) collective-permute-start(bf16[32,16,512]{2,1,0:T(8,128)(2,1)S(1)} %slice.94), channel_id=1, source_target_pairs={{0,6},{1,97},{2,4},{3,99},{4,2},{5,101},{6,0},{7,103},{8,14},{9,10... | collective-permute-start | bytes 1572872 | tf_op jit(solution)/shard_map/ppermute | solution.py:51
  66.4 50.0 %collective-permute-start.7 = (bf16[128,16,512]{2,1,0:T(8,128)(2,1)S(1)}, bf16[128,16,512]{2,1,0:T(8,128)(2,1)}, u32[]{:S(2)}, u32[]{:S(2)}) collective-permute-start(bf16[128,16,512]{2,1,0:T(8,128)(2,1)S(1)} %constant_dynamic-update-slice_fusion.18.own_ref), channel_id=1, source_target_pairs={{0,1},{1,0},{2,3},{3,2},{4,5},{5,4},{6,7},{7,6},{8,9},{9,8},{10,11... | collective-permute-start | bytes 6291464 | tf_op jit(solution)/shard_map/ppermute | solution.py:51
  74.6 25.6 %copy-start.9 = (f32[16,512]{1,0:T(8,128)S(1)}, f32[16,512]{1,0:T(8,128)}, u32[]{:S(2)}) copy-start(f32[16,512]{1,0:T(8,128)} %param.12) | copy-start | bytes 98308
  74.6 25.6 %copy-start.10 = (f32[16,512]{1,0:T(8,128)S(1)}, f32[16,512]{1,0:T(8,128)}, u32[]{:S(2)}) copy-start(f32[16,512]{1,0:T(8,128)} %param.13) | copy-start | bytes 98308
  74.6 41.9 %copy-start.1 = (f32[4096]{0:T(1024)S(1)}, f32[4096]{0:T(1024)}, u32[]{:S(2)}) copy-start(f32[4096]{0:T(1024)} %param.10) | copy-start | bytes 49156
  74.6 41.9 %copy-start.3 = (bf16[512,512]{1,0:T(8,128)(2,1)S(1)}, bf16[512,512]{1,0:T(8,128)(2,1)}, u32[]{:S(2)}) copy-start(bf16[512,512]{1,0:T(8,128)(2,1)} %cot_ref.3) | copy-start | bytes 1572868
  74.6 41.9 %copy-start.5 = (s32[512]{0:T(512)S(1)}, s32[512]{0:T(512)}, u32[]{:S(2)}) copy-start(s32[512]{0:T(512)} %param.14) | copy-start | bytes 6148
  74.6 41.9 %copy-start.6 = (s32[2,256]{1,0:T(2,128)S(1)}, s32[2,256]{1,0:T(2,128)}, u32[]{:S(2)}) copy-start(s32[2,256]{1,0:T(2,128)} %constant.41.clone.off_ref) | copy-start | bytes 6148
  74.7 5.6 %collective-permute-start.11 = (bf16[16,16,512]{2,1,0:T(8,128)(2,1)S(1)}, bf16[16,16,512]{2,1,0:T(8,128)(2,1)S(1)}, u32[]{:S(2)}, u32[]{:S(2)}) collective-permute-start(bf16[16,16,512]{2,1,0:T(8,128)(2,1)S(1)} %slice.95), channel_id=1, source_target_pairs={{0,32},{1,3},{2,34},{3,1},{4,36},{5,7},{6,38},{7,5},{8,40},{9,11},... | collective-permute-start | bytes 786440 | tf_op jit(solution)/shard_map/ppermute | solution.py:51
  80.4 5.4 %collective-permute-start.12 = (bf16[8,16,512]{2,1,0:T(8,128)(2,1)S(1)}, bf16[8,16,512]{2,1,0:T(8,128)(2,1)S(1)}, u32[]{:S(2)}, u32[]{:S(2)}) collective-permute-start(bf16[8,16,512]{2,1,0:T(8,128)(2,1)S(1)} %slice.96), channel_id=1, source_target_pairs={{0,96},{1,7},{2,98},{3,5},{4,100},{5,3},{6,102},{7,1},{8,104},{9,1... | collective-permute-start | bytes 393224 | tf_op jit(solution)/shard_map/ppermute | solution.py:51
  85.9 5.7 %collective-permute-start.13 = (bf16[4,16,512]{2,1,0:T(8,128)(2,1)S(1)}, bf16[4,16,512]{2,1,0:T(8,128)(2,1)S(1)}, u32[]{:S(2)}, u32[]{:S(2)}) collective-permute-start(bf16[4,16,512]{2,1,0:T(8,128)(2,1)S(1)} %slice.97), channel_id=1, source_target_pairs={{0,152},{1,153},{2,154},{3,155},{4,156},{5,157},{6,158},{7,159},{8... | collective-permute-start | bytes 196616 | tf_op jit(solution)/shard_map/ppermute | solution.py:51
  91.6 5.0 %collective-permute-start.14 = (f32[2,16,512]{2,1,0:T(8,128)S(1)}, f32[2,16,512]{2,1,0:T(8,128)S(1)}, u32[]{:S(2)}, u32[]{:S(2)}) collective-permute-start(f32[2,16,512]{2,1,0:T(8,128)S(1)} %slice.72), channel_id=1, source_target_pairs={{0,136},{1,137},{2,138},{3,139},{4,140},{5,141},{6,142},{7,143},{8... | collective-permute-start | bytes 196616 | tf_op jit(solution)/shard_map/ppermute | solution.py:51
  96.6 3.6 %collective-permute-start.15 = (f32[1,16,512]{2,1,0:T(8,128)S(1)}, f32[1,16,512]{2,1,0:T(8,128)S(1)}, u32[]{:S(2)}, u32[]{:S(2)}) collective-permute-start(f32[1,16,512]{2,1,0:T(8,128)S(1)} %slice.74), channel_id=1, source_target_pairs={{0,128},{1,129},{2,130},{3,131},{4,132},{5,133},{6,134},{7,135},{8... | collective-permute-start | bytes 98312 | tf_op jit(solution)/shard_map/ppermute | solution.py:51
  101.7 27.6 %all-to-all-start = ((f32[256,1,16]{2,1,0:T(1,128)}), f32[256,1,16]{2,1,0:T(1,128)S(1)}, u32[]{:S(2)}, u32[]{:S(2)}) async-start(f32[256,1,16]{2,1,0:T(1,128)} %broadcast_in_dim.2), calls=%async_computation | async-start | bytes 262144 | tf_op jit(solution)/shard_map/all_to_all | solution.py:236

commit v2 on v1

v2 whole, which is shorter than its diff:
```python
import functools
import math

import jax
import jax.numpy as jnp
import numpy as np
from jax import lax
from jax.experimental import pallas as pl
from jax.experimental.pallas import tpu as pltpu
from jax.sharding import PartitionSpec as P

RESERVED = 256
STEP = 10

norm_epsilon = 1e-05
beta_one = 0.9
beta_two = 0.95
adam_epsilon = 1e-08
learning_rate = 0.001
weight_decay = 0.1

bf16 = jnp.bfloat16
f32 = jnp.float32
AXES = ("grp", "loc")
DEVICES = 256

CORE = 1
X1, X3, Y1, Y3 = 2, 6, 32, 96
Z1, Z2, Z6 = 128, 8, 24
A1, A3, B1, B3 = (X1, Y1), (X3, Y3), (Y1, X1), (Y3, X3)
A13, B13 = (X1 ^ X3, Y1 ^ Y3), (Y1 ^ Y3, X1 ^ X3)
HALVES = 2
PARTS = 2
CHUNKS = 4
STEPS = ((CORE, A1, A3, B1, B3, Z6, Z2, Z1), (CORE, A3, A1, B1, B3, Z6, Z2, Z1))


def mask_of(mask, core):
    return mask[core] if isinstance(mask, tuple) else mask


def offsets(steps, core):
    own, other = ([0], [0])
    for mask in steps[:0:-1]:
        own = own + [o ^ mask_of(mask, core) for o in own]
        other = other + [o ^ mask_of(mask, 1 - core) for o in other]
    return own + [o ^ CORE for o in other]


OFFSET_OF = np.array([[offsets(s, 0), offsets(s, 1)] for s in STEPS], np.int32)
POSITION_OF = np.argsort(OFFSET_OF, axis=2).astype(np.int32)
TABLE = np.concatenate([POSITION_OF.reshape(-1), OFFSET_OF.reshape(-1)])


def position(table_ref, which, core, offset):
    return table_ref[(2 * which + core) * DEVICES + offset]


def offset_at(table_ref, which, core, place):
    return table_ref[(2 * HALVES + 2 * which + core) * DEVICES + place]


def exchange(x, mask):
    pairs = [(i, i ^ mask_of(mask, i & 1)) for i in range(DEVICES)]
    return lax.ppermute(x, AXES, pairs)


def column(row):
    return jnp.transpose(jnp.broadcast_to(row, (8, row.shape[1])))[:, :1]


def params(mib):
    return pltpu.CompilerParams(vmem_limit_bytes=mib * 2**20)


VMEM = pl.BlockSpec(memory_space=pltpu.VMEM)
SMEM = pl.BlockSpec(memory_space=pltpu.SMEM)


def grad_kernel(me_ref, table_hbm, h_hbm, gain_hbm, cot_hbm, ids_hbm, inv_ref, masked_ref, keep0_ref, send0_ref, keep1_ref, send1_ref, table_ref, h_ref, gain_ref, cot_ref, ids_ref, normed_ref, blk_ref, sems):
    tokens, features = h_ref.shape
    rows = tokens // CHUNKS
    me = me_ref[0]
    core = jnp.bitwise_and(me, 1)
    small = [
        pltpu.make_async_copy(source, target, sems.at[CHUNKS + i])
        for i, (source, target) in enumerate(
            ((ids_hbm, ids_ref), (gain_hbm, gain_ref), (cot_hbm, cot_ref), (table_hbm, table_ref))
        )
    ]
    copies = []
    for c in range(CHUNKS):
        at = pl.ds(c * rows, rows)
        copies.append(pltpu.make_async_copy(h_hbm.at[at], h_ref.at[at], sems.at[c]))
    small[0].start()
    small[1].start()
    copies[0].start()
    small[2].start()
    small[3].start()
    for copy in copies[1:]:
        copy.start()
    for copy in small:
        copy.wait()
    live = column(ids_ref[...]) >= RESERVED
    masked = jnp.where(live, cot_ref[...], jnp.zeros_like(cot_ref))
    masked_ref[...] = masked
    for c, copy in enumerate(copies):
        copy.wait()
        of = slice(c * rows, c * rows + rows)
        total = jnp.zeros((rows, 128), f32)
        for j in range(features // 128):
            x = h_ref[of, 128 * j : 128 * j + 128].astype(f32)
            total = total + x * x
        mean = jnp.sum(total, axis=1, keepdims=True) * (1.0 / features)
        inv = lax.rsqrt(mean + norm_epsilon)
        inv_ref[of, :] = inv
        for j in range(features // 512):
            at = slice(512 * j, 512 * j + 512)
            normed = ((h_ref[of, at].astype(f32) * inv) * gain_ref[:, at]).astype(bf16)
            normed_ref[at, of] = jnp.transpose(normed)
    width = blk_ref.shape[1] * blk_ref.shape[2]
    wide = keep0_ref.shape[2]
    for j in range(features // width):
        slot = j % 2
        part = jnp.dot(
            normed_ref[j * width : (j + 1) * width, :], masked, preferred_element_type=f32
        )
        blk_ref[slot] = part.reshape(blk_ref.shape[1:])
        first = j * (width // 16)
        for i in range(width // 32):
            own = 2 * i + core
            away = 2 * i + (1 - core)
            for which, keep_ref, send_ref in ((0, keep0_ref, send0_ref), (1, keep1_ref, send1_ref)):
                at = slice(which * wide, which * wide + wide)
                p = position(table_ref, which, core, jnp.bitwise_xor(first + own, me))
                q = position(table_ref, which, core, jnp.bitwise_xor(first + away, me))
                keep_ref[p] = blk_ref[slot, own, :, at]
                send_ref[q - DEVICES // 2] = blk_ref[slot, away, :, at].astype(bf16)


def local_grad(me, table, hidden, gain, cot, ids):
    tokens, features = hidden.shape
    outs = cot.shape[1]
    half = features // 32
    keep = jax.ShapeDtypeStruct((half, 16, outs // HALVES), f32)
    send = jax.ShapeDtypeStruct((half, 16, outs // HALVES), bf16)
    return pl.pallas_call(
        grad_kernel,
        out_shape=(
            jax.ShapeDtypeStruct((tokens, 1), f32),
            jax.ShapeDtypeStruct((tokens, outs), bf16),
            keep,
            send,
            keep,
            send,
        ),
        in_specs=[SMEM] + [pl.BlockSpec(memory_space=pltpu.HBM)] * 5,
        out_specs=(VMEM,) * 6,
        scratch_shapes=[
            pltpu.SMEM(table.shape, jnp.int32),
            pltpu.VMEM((tokens, features), bf16),
            pltpu.VMEM((1, features), f32),
            pltpu.VMEM((tokens, outs), bf16),
            pltpu.VMEM((1, tokens), jnp.int32),
            pltpu.VMEM((features, tokens), bf16),
            pltpu.VMEM((2, 32, 16, outs), f32),
            pltpu.SemaphoreType.DMA((CHUNKS + 4,)),
        ],
        compiler_params=params(46),
        cost_estimate=pl.CostEstimate(
            flops=2 * tokens * features * outs, bytes_accessed=12 * 2**20, transcendentals=0
        ),
        name="local_grad",
    )(me, table, hidden, gain, cot, ids)


def split_kernel(keep_ref, got_ref, kept_ref, leave_ref):
    half = kept_ref.shape[0]
    kept_ref[...] = keep_ref[:half] + got_ref[:half].astype(f32)
    leave_ref[...] = (keep_ref[half:] + got_ref[half:].astype(f32)).astype(bf16)


def split(keep, got):
    blocks, rows, outs = keep.shape
    return pl.pallas_call(
        split_kernel,
        out_shape=(
            jax.ShapeDtypeStruct((blocks // 2, rows, outs), f32),
            jax.ShapeDtypeStruct((blocks // 2, rows, outs), bf16),
        ),
        in_specs=[VMEM, VMEM],
        out_specs=(VMEM, VMEM),
        compiler_params=params(6),
        name="split",
    )(keep, got)


def merge_kernel(me_ref, table_ref, keep0_ref, got0_ref, keep1_ref, got1_ref, w_ref, keep_ref, send_ref, gain_ref):
    blocks = w_ref.shape[0]
    wide = keep0_ref.shape[2]
    me = me_ref[0]
    core = jnp.bitwise_and(me, 1)
    lane = lax.broadcasted_iota(jnp.int32, (16, 128), 1)
    gain = jnp.zeros((16, 128), f32)
    for p in range(blocks):
        left = keep0_ref[p] + got0_ref[p].astype(f32)
        right = keep1_ref[p] + got1_ref[p].astype(f32)
        w = w_ref[p].astype(f32)
        prod = left * w[:, :wide] + right * w[:, wide:]
        row = jnp.sum(prod, axis=1, keepdims=True)
        at = jnp.bitwise_xor(offset_at(table_ref, 0, core, p), me) // 2
        gain = gain + jnp.where(lane == at, row, 0.0)
        if p < blocks // 2:
            keep_ref[p, :, :wide] = left
            keep_ref[p, :, wide:] = right
        else:
            send_ref[p - blocks // 2, :, :wide] = left.astype(bf16)
            send_ref[p - blocks // 2, :, wide:] = right.astype(bf16)
    gain_ref[...] = gain


def merge(me, table, keep0, got0, keep1, got1, w):
    blocks, rows, outs = w.shape
    return pl.pallas_call(
        merge_kernel,
        out_shape=(
            jax.ShapeDtypeStruct((blocks // 2, rows, outs), f32),
            jax.ShapeDtypeStruct((blocks // 2, rows, outs), bf16),
            jax.ShapeDtypeStruct((rows, 128), f32),
        ),
        in_specs=[SMEM, SMEM] + [VMEM] * 5,
        out_specs=(VMEM, VMEM, VMEM),
        compiler_params=params(8),
        name="merge",
    )(me, table, keep0, got0, keep1, got1, w)


def place_kernel(me_ref, table_ref, own0_ref, other0_ref, own1_ref, other1_ref, w_ref):
    me = me_ref[0]
    core = jnp.bitwise_and(me, 1)
    half = DEVICES // 2
    wide = own0_ref.shape[2]

    def place(p, carry):
        for which, own_ref, other_ref in ((0, own0_ref, other0_ref), (1, own1_ref, other1_ref)):
            columns = slice(which * wide, which * wide + wide)
            near = jnp.bitwise_xor(offset_at(table_ref, which, core, p), me)
            far = jnp.bitwise_xor(offset_at(table_ref, which, core, p + half), me)
            w_ref[near, :, columns] = own_ref[p]
            w_ref[far, :, columns] = other_ref[p]
        return carry

    lax.fori_loop(0, half, place, 0, unroll=8)


def whole_weight(me, table, pieces):
    blocks, rows, wide = pieces[0].shape
    return pl.pallas_call(
        place_kernel,
        out_shape=jax.ShapeDtypeStruct((2 * blocks, rows, HALVES * wide), bf16),
        in_specs=[SMEM, SMEM] + [VMEM] * 4,
        out_specs=VMEM,
        compiler_params=params(10),
        name="whole_weight",
    )(me, table, *pieces)


def both_kernel(h_ref, inv_ref, gain_ref, masked_ref, w_ref, *refs):
    values_ref, grad_ref, wt_ref = refs[-3:]
    tokens, features = h_ref.shape
    width = 512
    inv = inv_ref[...]
    masked = masked_ref[...]
    values = jnp.zeros(values_ref.shape, f32)
    inner = jnp.zeros((tokens, 128), f32)
    for j in range(features // width):
        at = slice(j * width, j * width + width)
        w = w_ref[j * (width // 16) : (j + 1) * (width // 16)].reshape(width, w_ref.shape[2])
        gain = gain_ref[:, at]
        scaled = h_ref[:, at].astype(f32) * inv
        values = values + jnp.dot((scaled * gain).astype(bf16), w, preferred_element_type=f32)
        back = lax.dot_general(masked, w, (((1,), (1,)), ((), ())), preferred_element_type=f32)
        weighted = back * gain
        wt_ref[:, at] = weighted
        prod = weighted * scaled
        for k in range(width // 128):
            inner = inner + prod[:, 128 * k : 128 * k + 128]
    values_ref[...] = values.astype(bf16)
    mean = jnp.sum(inner, axis=1, keepdims=True) * (1.0 / features)
    for j in range(features // width):
        at = slice(j * width, j * width + width)
        scaled = h_ref[:, at].astype(f32) * inv
        grad_ref[:, at] = ((wt_ref[:, at] - scaled * mean) * inv).astype(bf16)


def values_and_input_grad(hidden, inv, gain, masked, weight, part, made):
    tokens, features = hidden.shape
    outs = masked.shape[1]
    rows = tokens // PARTS
    left = pl.BlockSpec(memory_space=pl.ANY)
    return pl.pallas_call(
        both_kernel,
        grid=(1,),
        out_shape=(
            jax.ShapeDtypeStruct((tokens, outs), bf16),
            jax.ShapeDtypeStruct((tokens, features), bf16),
        ),
        in_specs=[
            pl.BlockSpec((rows, features), lambda i: (i + part, 0)),
            pl.BlockSpec((rows, 1), lambda i: (i + part, 0)),
            pl.BlockSpec((1, features), lambda i: (0, 0)),
            pl.BlockSpec((rows, outs), lambda i: (i + part, 0)),
            VMEM,
        ]
        + [left] * len(made),
        out_specs=(
            pl.BlockSpec((rows, outs), lambda i: (i + part, 0)),
            pl.BlockSpec((rows, features), lambda i: (i + part, 0)),
        ),
        scratch_shapes=[pltpu.VMEM((rows, features), f32)],
        input_output_aliases={5 + i: i for i in range(len(made))},
        compiler_params=params(16),
        cost_estimate=pl.CostEstimate(
            flops=4 * rows * features * outs, bytes_accessed=6 * 2**20, transcendentals=0
        ),
        name="values_and_input_grad",
    )(hidden, inv, gain, masked, weight, *made)


together = lax.optimization_barrier


def grow(held, got):
    return jnp.concatenate([held, got], axis=0)


def unpack(got):
    blocks, last = got[:-1].astype(f32), got[-1].astype(f32)
    return blocks, (last[:, :128] + last[:, 128:256]) + last[:, 256:384]


def pack(blocks, gain):
    high = gain.astype(bf16)
    rest = gain - high.astype(f32)
    middle = rest.astype(bf16)
    low = (rest - middle.astype(f32)).astype(bf16)
    last = jnp.concatenate([high, middle, low, jnp.zeros_like(low)], axis=1)
    return jnp.concatenate([blocks.astype(bf16), last[None]], axis=0)


def unpack_wide(got):
    last = got[-1]
    return got[:-1], jnp.concatenate([last[:, :128], last[:, 128:256]], axis=0)


def pack_wide(blocks, gain):
    rows = gain.shape[0] // 2
    last = jnp.concatenate([gain[:rows], gain[rows:]], axis=1)
    last = jnp.pad(last, ((0, 0), (0, blocks.shape[2] - last.shape[1])))
    return jnp.concatenate([blocks, last[None]], axis=0)


def shards(
    hidden_states, norm_gain, master_weight, first_moment, second_moment, token_ids, out_cotangent
):
    tokens_all = hidden_states.shape[0] * DEVICES
    grad_scale = 1.0 / math.sqrt(tokens_all)
    features = hidden_states.shape[1]
    rows, outs = master_weight.shape
    wide = outs // HALVES
    index = lax.axis_index("grp") * lax.axis_size("loc") + lax.axis_index("loc")
    me = index.astype(jnp.int32).reshape(1)
    table = jnp.asarray(TABLE)
    gain_row = norm_gain.reshape(1, features)
    ids_row = token_ids.reshape(1, -1)

    held = master_weight.astype(bf16).reshape(1, rows, outs)
    got = exchange(held, Z1)
    inv, masked, keep0, send0, keep1, send1 = local_grad(
        me, table, hidden_states, gain_row, out_cotangent, ids_row
    )
    held, got, send0, send1 = together((held, got, send0, send1))

    held = grow(held, got)
    swap0 = exchange(send0, CORE)
    swap1 = exchange(send1, CORE)
    got = exchange(held, Z2)
    got, swap0, swap1 = together((got, swap0, swap1))

    held = grow(held, got)
    keep0, send0 = split(keep0, swap0)
    keep1, send1 = split(keep1, swap1)
    held, send0, send1 = together((held, send0, send1))
    got0, got1 = exchange(send0, A1), exchange(send1, A3)
    held = grow(held, exchange(held, Z6))
    got = exchange(held, B3)
    got, got0, got1 = together((got, got0, got1))

    held = grow(held, got)
    keep0, send0 = split(keep0, got0)
    keep1, send1 = split(keep1, got1)
    held, send0, send1 = together((held, send0, send1))
    got = exchange(held, B1)
    got0, got1 = exchange(send0, A3), exchange(send1, A1)
    held = grow(held, got)
    part0, part1 = held[:, :, :wide], held[:, :, wide:]
    more0, more1 = exchange(part0, A3), exchange(part1, A1)

    part0, part1 = grow(part0, more0), grow(part1, more1)
    keep, send, gain = merge(me, table, keep0, got0, keep1, got1, held)
    got = exchange(send, B1)
    more0, more1 = exchange(part0, A1), exchange(part1, A3)
    near, next_to, across = exchange(gain, A1), exchange(gain, A3), exchange(gain, A13)
    gain = (gain + near) + (next_to + across)

    part0, part1 = grow(part0, more0), grow(part1, more1)
    more0, more1 = exchange(part0, CORE), exchange(part1, CORE)
    total = keep + got.astype(f32)
    half = total.shape[0] // 2
    keep, got = total[:half], exchange(pack(total[half:], gain), B3)
    near, across = exchange(gain, B1), exchange(gain, B13)

    weight = whole_weight(me, table, (part0, more0, part1, more1))

    def finish(part, made=()):
        return values_and_input_grad(hidden_states, inv, gain_row, masked, weight, part, made)

    blocks, other = unpack(got)
    total, gain = keep + blocks, (gain + near) + (other + across)
    half = total.shape[0] // 2
    keep, got = total[:half], exchange(pack(total[half:], gain), Z6)
    near, across = exchange(gain, CORE), exchange(gain, CORE ^ Z6)
    made = finish(0)
    got, made = together((got, made))

    blocks, other = unpack(got)
    total, mine, other = keep + blocks, gain + other, near + across
    core = jnp.bitwise_and(index, 1)
    gain = jnp.concatenate(
        [jnp.where(core == 0, mine, other), jnp.where(core == 0, other, mine)], axis=0
    )
    half = total.shape[0] // 2
    keep, got = total[:half], exchange(pack_wide(total[half:], gain), Z2)
    made = finish(1, made)
    got, made = together((got, made))
    value_heads, input_grad = made

    blocks, other = unpack_wide(got)
    total, gain = keep + blocks, gain + other
    half = total.shape[0] // 2
    got = exchange(pack_wide(total[half:], gain), Z1)
    blocks, other = unpack_wide(got)
    total, gain = total[:half] + blocks, gain + other
    summed = total.reshape(rows, outs)

    gain_grad = jnp.transpose(gain).reshape(features) * grad_scale / norm_gain

    weight_grad = summed * grad_scale
    new_first = beta_one * first_moment + (1.0 - beta_one) * weight_grad
    new_second = beta_two * second_moment + (1.0 - beta_two) * weight_grad * weight_grad
    first_bias = 1.0 - beta_one**STEP
    second_bias = 1.0 - beta_two**STEP
    update = new_first / first_bias / (jnp.sqrt(new_second / second_bias) + adam_epsilon)
    new_master = master_weight - learning_rate * (update + weight_decay * master_weight)
    return (value_heads, input_grad, gain_grad, new_master, new_first, new_second)


def solution(mesh):
    in_specs = (
        P(("grp", "loc"), None),
        P(),
        P(("grp", "loc"), None),
        P(("grp", "loc"), None),
        P(("grp", "loc"), None),
        P(("grp", "loc")),
        P(("grp", "loc"), None),
    )
    out_specs = (
        P(("grp", "loc"), None),
        P(("grp", "loc"), None),
        P(),
        P(("grp", "loc"), None),
        P(("grp", "loc"), None),
        P(("grp", "loc"), None),
    )
    return jax.shard_map(shards, mesh=mesh, in_specs=in_specs, out_specs=out_specs, check_vma=False)
```

time: 132 us -> 97.1 us (0.74)
  waiting for transfers between devices: 46.7 us -> 21.5 us
  other arithmetic: 6.09 us -> 2.7 us
  Pallas kernels: 22.3 us -> 19.2 us
  starting transfers between devices: 50.3 us -> 48.7 us
  local copies, waits for them, and re-layouts: 5.1 us -> 3.6 us
    ppermute x16 -> x29, waiting for transfers between devices: 46.1 us -> 21.5 us  [exchange(): return lax.ppermute(x, AXES, pairs)]
    all_to_all x1 -> x0, starting transfers between devices: 14.8 us -> none  [shards(): lax.all_to_all(jnp.broadcast_to(gain_rows, (DEVICES, rows)), AXES, split_...]
    ppermute x16 -> x29, starting transfers between devices: 35.5 us -> 48.7 us  [exchange(): return lax.ppermute(x, AXES, pairs)]
    pallas_call x1, Pallas kernels: 10.1 us -> 6.47 us  [local_grad(): pl.pallas_call(grad_kernel, out_shape=(jax.ShapeDtypeStruct((tokens, 1),...]
    add x7 -> x5, other arithmetic: 3.7 us -> 0.16 us  [the longest x1 0.09 us: shards(): total = keep + got.astype(f32)]
    pallas_call x1 -> x8, Pallas kernels: 12.1 us -> 12.7 us  [the longest x2 9.51 us: values_and_input_grad(): pl.pallas_call(both_kernel, grid=(1,), out_shape=(jax.ShapeDtypeStruct((t...]
    unnamed x28 -> x21, local copies, waits for them, and re-layouts: 3.3 us -> 3.3 us
  transfers between devices with their start and end apart: 17 -> 29, of which waited for: 14 -> 9; matrix products, arithmetic and copies ran while one was open for 4% -> 1% of each run, Pallas kernels for 9% -> 18%
where the time goes in v2:
time: 97.1 us; the launch traced here: 96.7 us
  starting transfers between devices  48.7 us (50%)
  waiting for transfers between devices  21.5 us (22%)
  Pallas kernels  19.2 us (20%)
  local copies, waits for them, and re-layouts  3.6 us (4%)
  other arithmetic  2.7 us (3%)
  between operations  1.07 us (1%)
    ppermute x29, starting transfers between devices, exchange(): return lax.ppermute(x, AXES, pairs)  48.7 us
    ppermute x29, waiting for transfers between devices, exchange(): return lax.ppermute(x, AXES, pairs)  21.5 us
    pallas_call x2, Pallas kernels, values_and_input_grad(): pl.pallas_call(both_kernel, grid=(1,), out_shape=(jax.ShapeDtypeStruct((t...  9.51 us
    pallas_call x1, Pallas kernels, local_grad(): pl.pallas_call(grad_kernel, out_shape=(jax.ShapeDtypeStruct((tokens, 1),...  6.47 us
    unnamed x21, local copies, waits for them, and re-layouts  3.3 us
  transfers between devices with their start and end apart: 29, of which 9 were waited for; matrix products, arithmetic and copies ran while one was open for 1% of the time, Pallas kernels for 18%

profile of v2, /device:TPU:1, one launch (start us, length us, event | category | flops | bytes accessed | tf_op | source)
XLA Modules:
  0.0 96.7 jit_solution(13392866134522567739)
XLA Ops:
  1.4 2.5 %collective-permute-start = (bf16[1,16,512]{2,1,0:T(8,128)(2,1)S(1)}, bf16[1,16,512]{2,1,0:T(8,128)(2,1)S(1)}, u32[]{:S(2)}, u32[]{:S(2)}) collective-permute-start(bf16[1,16,512]{2,1,0:T(8,128)(2,1)S(1)} %convert_bitcast_fusion), channel_id=1, source_target_pairs={{0,128},{1,129},{2,130},{3,131},{4,132},{5,133},{6,134},{7,135},{8... | collective-permute-start | bytes 49160 | tf_op jit(solution)/shard_map/ppermute | solution.py:65
  5.3 1.0 %copy-done.5 = bf16[512,512]{1,0:T(8,128)(2,1)S(1)} copy-done((bf16[512,512]{1,0:T(8,128)(2,1)S(1)}, bf16[512,512]{1,0:T(8,128)(2,1)}, u32[]{:S(2)}) %copy-start.5) | copy-done | bytes 524312
  7.0 6.5 %local_grad.1 = (f32[512,1]{1,0:T(8,128)S(1)}, bf16[512,512]{1,0:T(8,128)(2,1)S(1)}, f32[128,16,256]{2,1,0:T(8,128)S(1)}, bf16[128,16,256]{2,1,0:T(8,128)(2,1)S(...) custom-call(s32[1]{0:T(128)} %bitcast.me_ref, s32[2048]{0:T(1024)S(1)} %copy-done.3, ...), custom_call_target="tpu_custom_call" | custom-call | flops 2147483648 | bytes 12582912 | tf_op jit(solution)/shard_map/local_grad/pallas_call | solution.py:147
  13.5 1.0 %collective-permute-start.2 = (bf16[128,16,256]{2,1,0:T(8,128)(2,1)S(1)}, bf16[128,16,256]{2,1,0:T(8,128)(2,1)S(1)}, u32[]{:S(2)}, u32[]{:S(2)}) collective-permute-start(bf16[128,16,256]{2,1,0:T(8,128)(2,1)S(1)} %get-tuple-element.54), channel_id=1, source_target_pairs={{0,1},{1,0},{2,3},{3,2},{4,5},{5,4},{6,7},{7,6},{8,9},{9,8},{10,11... | collective-permute-start | bytes 3145736 | tf_op jit(solution)/shard_map/ppermute | solution.py:65
  14.6 3.0 %collective-permute-start.1 = (bf16[2,16,512]{2,1,0:T(8,128)(2,1)S(1)}, bf16[2,16,512]{2,1,0:T(8,128)(2,1)S(1)}, u32[]{:S(2)}, u32[]{:S(2)}) collective-permute-start(bf16[2,16,512]{2,1,0:T(8,128)(2,1)S(1)} %pad_maximum_fusion.11), channel_id=1, source_target_pairs={{0,8},{1,9},{2,10},{3,11},{4,12},{5,13},{6,14},{7,15},{8,0},{9,1},... | collective-permute-start | bytes 98312 | tf_op jit(solution)/shard_map/ppermute | solution.py:65
  17.6 1.3 %collective-permute-done.1 = bf16[2,16,512]{2,1,0:T(8,128)(2,1)S(1)} collective-permute-done((bf16[2,16,512]{2,1,0:T(8,128)(2,1)S(1)}, bf16[2,16,512]{2,1,0:T(8,128)(2,1)S(1)}, u32[]{:S(2)}, u32[]{:S(2)}) %collective-permute-start.1) | collective-permute-done | bytes 32800 | tf_op jit(solution)/shard_map/ppermute | solution.py:65
  19.3 2.1 %collective-permute-start.6 = (bf16[64,16,256]{2,1,0:T(8,128)(2,1)S(1)}, bf16[64,16,256]{2,1,0:T(8,128)(2,1)S(1)}, u32[]{:S(2)}, u32[]{:S(2)}) collective-permute-start(bf16[64,16,256]{2,1,0:T(8,128)(2,1)S(1)} %get-tuple-element.64), channel_id=1, source_target_pairs={{0,2},{1,33},{2,0},{3,35},{4,6},{5,37},{6,4},{7,39},{8,10},{9,41},... | collective-permute-start | bytes 1572872 | tf_op jit(solution)/shard_map/ppermute | solution.py:65
  21.5 1.9 %collective-permute-start.7 = (bf16[64,16,256]{2,1,0:T(8,128)(2,1)S(1)}, bf16[64,16,256]{2,1,0:T(8,128)(2,1)S(1)}, u32[]{:S(2)}, u32[]{:S(2)}) collective-permute-start(bf16[64,16,256]{2,1,0:T(8,128)(2,1)S(1)} %get-tuple-element.65), channel_id=1, source_target_pairs={{0,6},{1,97},{2,4},{3,99},{4,2},{5,101},{6,0},{7,103},{8,14},{9,10... | collective-permute-start | bytes 1572872 | tf_op jit(solution)/shard_map/ppermute | solution.py:65
  23.4 3.8 %collective-permute-start.4 = (bf16[4,16,512]{2,1,0:T(8,128)(2,1)S(1)}, bf16[4,16,512]{2,1,0:T(8,128)(2,1)S(1)}, u32[]{:S(2)}, u32[]{:S(2)}) collective-permute-start(bf16[4,16,512]{2,1,0:T(8,128)(2,1)S(1)} %pad_maximum_fusion.9), channel_id=1, source_target_pairs={{0,24},{1,25},{2,26},{3,27},{4,28},{5,29},{6,30},{7,31},{8,16},{9,... | collective-permute-start | bytes 196616 | tf_op jit(solution)/shard_map/ppermute | solution.py:65
  27.1 1.8 %collective-permute-done.4 = bf16[4,16,512]{2,1,0:T(8,128)(2,1)S(1)} collective-permute-done((bf16[4,16,512]{2,1,0:T(8,128)(2,1)S(1)}, bf16[4,16,512]{2,1,0:T(8,128)(2,1)S(1)}, u32[]{:S(2)}, u32[]{:S(2)}) %collective-permute-start.4) | collective-permute-done | bytes 65568 | tf_op jit(solution)/shard_map/ppermute | solution.py:65
  28.9 3.0 %collective-permute-start.5 = (bf16[8,16,512]{2,1,0:T(8,128)(2,1)S(1)}, bf16[8,16,512]{2,1,0:T(8,128)(2,1)S(1)}, u32[]{:S(2)}, u32[]{:S(2)}) collective-permute-start(bf16[8,16,512]{2,1,0:T(8,128)(2,1)S(1)} %pad_maximum_fusion.6), channel_id=1, source_target_pairs={{0,96},{1,7},{2,98},{3,5},{4,100},{5,3},{6,102},{7,1},{8,104},{9,1... | collective-permute-start | bytes 393224 | tf_op jit(solution)/shard_map/ppermute | solution.py:65
  31.9 2.4 %collective-permute-done.5 = bf16[8,16,512]{2,1,0:T(8,128)(2,1)S(1)} collective-permute-done((bf16[8,16,512]{2,1,0:T(8,128)(2,1)S(1)}, bf16[8,16,512]{2,1,0:T(8,128)(2,1)S(1)}, u32[]{:S(2)}, u32[]{:S(2)}) %collective-permute-start.5) | collective-permute-done | bytes 131104 | tf_op jit(solution)/shard_map/ppermute | solution.py:65
  34.5 1.0 %collective-permute-start.10 = (bf16[16,16,512]{2,1,0:T(8,128)(2,1)S(1)}, bf16[16,16,512]{2,1,0:T(8,128)(2,1)S(1)}, u32[]{:S(2)}, u32[]{:S(2)}) collective-permute-start(bf16[16,16,512]{2,1,0:T(8,128)(2,1)S(1)} %pad_maximum_fusion.4), channel_id=1, source_target_pairs={{0,32},{1,3},{2,34},{3,1},{4,36},{5,7},{6,38},{7,5},{8,40},{9,11},... | collective-permute-start | bytes 786440 | tf_op jit(solution)/shard_map/ppermute | solution.py:65
  35.5 1.3 %collective-permute-start.8 = (bf16[32,16,256]{2,1,0:T(8,128)(2,1)S(1)}, bf16[32,16,256]{2,1,0:T(8,128)(2,1)S(1)}, u32[]{:S(2)}, u32[]{:S(2)}) collective-permute-start(bf16[32,16,256]{2,1,0:T(8,128)(2,1)S(1)} %get-tuple-element.73), channel_id=1, source_target_pairs={{0,6},{1,97},{2,4},{3,99},{4,2},{5,101},{6,0},{7,103},{8,14},{9,10... | collective-permute-start | bytes 786440 | tf_op jit(solution)/shard_map/ppermute | solution.py:65
  36.8 3.0 %collective-permute-done.10 = bf16[16,16,512]{2,1,0:T(8,128)(2,1)S(1)} collective-permute-done((bf16[16,16,512]{2,1,0:T(8,128)(2,1)S(1)}, bf16[16,16,512]{2,1,0:T(8,128)(2,1)S(1)}, u32[]{:S(2)}, u32[]{:S(2)}) %collective-permute-start.10) | collective-permute-done | bytes 262176 | tf_op jit(solution)/shard_map/ppermute | solution.py:65
  39.8 2.1 %collective-permute-done.8.got0_ref = bf16[32,16,256]{2,1,0:T(8,128)(2,1)S(1)} collective-permute-done((bf16[32,16,256]{2,1,0:T(8,128)(2,1)S(1)}, bf16[32,16,256]{2,1,0:T(8,128)(2,1)S(1)}, u32[]{:S(2)}, u32[]{:S(2)}) %collective-permute-start.8) | collective-permute-done | bytes 262176 | tf_op jit(solution)/shard_map/ppermute | solution.py:65
  41.9 1.1 %collective-permute-done.9.got1_ref = bf16[32,16,256]{2,1,0:T(8,128)(2,1)S(1)} collective-permute-done((bf16[32,16,256]{2,1,0:T(8,128)(2,1)S(1)}, bf16[32,16,256]{2,1,0:T(8,128)(2,1)S(1)}, u32[]{:S(2)}, u32[]{:S(2)}) %collective-permute-start.9) | collective-permute-done | bytes 262176 | tf_op jit(solution)/shard_map/ppermute | solution.py:65
  43.0 1.0 merge.1
  44.2 2.2 %collective-permute-start.13 = (f32[16,128]{1,0:T(8,128)S(1)}, f32[16,128]{1,0:T(8,128)S(1)}, u32[]{:S(2)}, u32[]{:S(2)}) collective-permute-start(f32[16,128]{1,0:T(8,128)S(1)} %get-tuple-element.79), channel_id=1, source_target_pairs={{0,6},{1,97},{2,4},{3,99},{4,2},{5,101},{6,0},{7,103},{8,14},{9,10... | collective-permute-start | bytes 24584 | tf_op jit(solution)/shard_map/ppermute | solution.py:65
  46.8 1.2 %collective-permute-start.22 = (bf16[32,16,256]{2,1,0:T(8,128)(2,1)S(1)}, bf16[32,16,256]{2,1,0:T(8,128)(2,1)S(1)}, u32[]{:S(2)}, u32[]{:S(2)}) collective-permute-start(bf16[32,16,256]{2,1,0:T(8,128)(2,1)S(1)} %get-tuple-element.101), channel_id=1, source_target_pairs={{0,2},{1,33},{2,0},{3,35},{4,6},{5,37},{6,4},{7,39},{8,10},{9,41},... | collective-permute-start | bytes 786440 | tf_op jit(solution)/shard_map/ppermute | solution.py:65
  48.4 2.3 %collective-permute-start.11 = (bf16[16,16,512]{2,1,0:T(8,128)(2,1)S(1)}, bf16[16,16,512]{2,1,0:T(8,128)(2,1)S(1)}, u32[]{:S(2)}, u32[]{:S(2)}) collective-permute-start(bf16[16,16,512]{2,1,0:T(8,128)(2,1)S(1)} %get-tuple-element.78), channel_id=1, source_target_pairs={{0,32},{1,3},{2,34},{3,1},{4,36},{5,7},{6,38},{7,5},{8,40},{9,11},... | collective-permute-start | bytes 786440 | tf_op jit(solution)/shard_map/ppermute | solution.py:65
  51.4 4.4 %collective-permute-start.17 = (f32[16,128]{1,0:T(8,128)S(1)}, f32[16,128]{1,0:T(8,128)S(1)}, u32[]{:S(2)}, u32[]{:S(2)}) collective-permute-start(f32[16,128]{1,0:T(8,128)S(1)} %get-tuple-element.100), channel_id=1, source_target_pairs={{0,64},{1,5},{2,66},{3,7},{4,68},{5,1},{6,70},{7,3},{8,72},{9,13},... | collective-permute-start | bytes 24584 | tf_op jit(solution)/shard_map/ppermute | solution.py:65
  56.6 5.0 %collective-permute-start.15 = (bf16[9,16,512]{2,1,0:T(8,128)(2,1)S(1)}, bf16[9,16,512]{2,1,0:T(8,128)(2,1)S(1)}, u32[]{:S(2)}, u32[]{:S(2)}) collective-permute-start(bf16[9,16,512]{2,1,0:T(8,128)(2,1)S(1)} %pad_maximum_fusion.5), channel_id=1, source_target_pairs={{0,96},{1,7},{2,98},{3,5},{4,100},{5,3},{6,102},{7,1},{8,104},{9,1... | collective-permute-start | bytes 442376 | tf_op jit(solution)/shard_map/ppermute | solution.py:65
  61.6 5.1 %collective-permute-done.20 = bf16[64,16,256]{2,1,0:T(8,128)(2,1)S(1)} collective-permute-done((bf16[64,16,256]{2,1,0:T(8,128)(2,1)S(1)}, bf16[64,16,256]{2,1,0:T(8,128)(2,1)S(1)}, u32[]{:S(2)}, u32[]{:S(2)}) %collective-permute-start.20) | collective-permute-done | bytes 524320 | tf_op jit(solution)/shard_map/ppermute | solution.py:65
  66.8 4.9 %collective-permute-start.21 = (bf16[128,16,256]{2,1,0:T(8,128)(2,1)S(1)}, bf16[128,16,256]{2,1,0:T(8,128)(2,1)S(1)}, u32[]{:S(2)}, u32[]{:S(2)}) collective-permute-start(bf16[128,16,256]{2,1,0:T(8,128)(2,1)S(1)} %pad_maximum_fusion.own0_ref), channel_id=1, source_target_pairs={{0,1},{1,0},{2,3},{3,2},{4,5},{5,4},{6,7},{7,6},{8,9},{9,8},{10,11... | collective-permute-start | bytes 3145736 | tf_op jit(solution)/shard_map/ppermute | solution.py:65
  72.6 4.3 %collective-permute-start.26 = (f32[16,128]{1,0:T(8,128)S(1)}, f32[16,128]{1,0:T(8,128)S(1)}, u32[]{:S(2)}, u32[]{:S(2)}) collective-permute-start(f32[16,128]{1,0:T(8,128)S(1)} %get-tuple-element.98), channel_id=1, source_target_pairs={{0,25},{1,24},{2,27},{3,26},{4,29},{5,28},{6,31},{7,30},{8,17},{9,... | collective-permute-start | bytes 24584 | tf_op jit(solution)/shard_map/ppermute | solution.py:65
  77.4 1.7 %whole_weight.1.w_ref = bf16[256,16,512]{2,1,0:T(8,128)(2,1)S(1)} custom-call(s32[1]{0:T(128)} %bitcast.me_ref, s32[2048]{0:T(1024)S(1)} %copy-done.4, bf16[128,16,256]{2,1,0:T(8,128)(2,1)S(1)} %pad_maximum_fusion.own0_ref, bf16[128,16,256]{2,1,0:T(8,128)(2,1)S(1)} %collective-permute-done.21.other0_ref, ...), custom_call_target="tpu_custom_call" | custom-call | tf_op jit(solution)/shard_map/whole_weight/pallas_call | solution.py:258
  79.3 4.8 %values_and_input_grad.2 = (bf16[512,512]{1,0:T(8,128)(2,1)}, bf16[512,4096]{1,0:T(8,128)(2,1)}) custom-call(bf16[512,4096]{1,0:T(8,128)(2,1)S(1)} %copy-done, f32[512,1]{1,0:T(8,128)S(1)} %get-tuple-element.80.inv_ref, f32[1,4096]{1,0:T(1,128)S(1)} %bitcast.34, bf16[512,512]{1,0:T(8,128)(2,1)S(1)} %get-tuple-element.81.masked_ref, ...), custom_call_target="tpu_custom_call" | custom-call | flops 2147483648 | bytes 6291456 | tf_op jit(solution)/shard_map/values_and_input_grad/pallas_call | solution.py:301
  84.2 1.4 %collective-permute-start.27 = (f32[3,16,512]{2,1,0:T(8,128)S(1)}, f32[3,16,512]{2,1,0:T(8,128)S(1)}, u32[]{:S(2)}, u32[]{:S(2)}) collective-permute-start(f32[3,16,512]{2,1,0:T(8,128)S(1)} %pad_maximum_fusion.7), channel_id=1, source_target_pairs={{0,8},{1,9},{2,10},{3,11},{4,12},{5,13},{6,14},{7,15},{8,0},{9,1},... | collective-permute-start | bytes 294920 | tf_op jit(solution)/shard_map/ppermute | solution.py:65
  85.6 4.8 %values_and_input_grad.3 = (bf16[512,512]{1,0:T(8,128)(2,1)}, bf16[512,4096]{1,0:T(8,128)(2,1)}) custom-call(bf16[512,4096]{1,0:T(8,128)(2,1)S(1)} %copy-done, f32[512,1]{1,0:T(8,128)S(1)} %get-tuple-element.80.inv_ref, f32[1,4096]{1,0:T(1,128)S(1)} %bitcast.35, ...), custom_call_target="tpu_custom_call", output_to_operand_aliasing={{0}: (5, {}), {1}: (6, {})} | custom-call | flops 2147483648 | bytes 6291456 | tf_op jit(solution)/shard_map/values_and_input_grad/pallas_call | solution.py:301
  90.3 1.5 %collective-permute-done.27 = f32[3,16,512]{2,1,0:T(8,128)S(1)} collective-permute-done((f32[3,16,512]{2,1,0:T(8,128)S(1)}, f32[3,16,512]{2,1,0:T(8,128)S(1)}, u32[]{:S(2)}, u32[]{:S(2)}) %collective-permute-start.27) | collective-permute-done | bytes 98336 | tf_op jit(solution)/shard_map/ppermute | solution.py:65
  92.1 3.1 %collective-permute-done.28 = f32[2,16,512]{2,1,0:T(8,128)S(1)} collective-permute-done((f32[2,16,512]{2,1,0:T(8,128)S(1)}, f32[2,16,512]{2,1,0:T(8,128)S(1)}, u32[]{:S(2)}, u32[]{:S(2)}) %collective-permute-start.28) | collective-permute-done | bytes 65568 | tf_op jit(solution)/shard_map/ppermute | solution.py:65
  (104 shorter events, 9.2 us)
Async XLA Ops:
  1.4 12.1 %collective-permute-start = (bf16[1,16,512]{2,1,0:T(8,128)(2,1)S(1)}, bf16[1,16,512]{2,1,0:T(8,128)(2,1)S(1)}, u32[]{:S(2)}, u32[]{:S(2)}) collective-permute-start(bf16[1,16,512]{2,1,0:T(8,128)(2,1)S(1)} %convert_bitcast_fusion), channel_id=1, source_target_pairs={{0,128},{1,129},{2,130},{3,131},{4,132},{5,133},{6,134},{7,135},{8... | collective-permute-start | bytes 49160 | tf_op jit(solution)/shard_map/ppermute | solution.py:65
  13.5 5.4 %collective-permute-start.2 = (bf16[128,16,256]{2,1,0:T(8,128)(2,1)S(1)}, bf16[128,16,256]{2,1,0:T(8,128)(2,1)S(1)}, u32[]{:S(2)}, u32[]{:S(2)}) collective-permute-start(bf16[128,16,256]{2,1,0:T(8,128)(2,1)S(1)} %get-tuple-element.54), channel_id=1, source_target_pairs={{0,1},{1,0},{2,3},{3,2},{4,5},{5,4},{6,7},{7,6},{8,9},{9,8},{10,11... | collective-permute-start | bytes 3145736 | tf_op jit(solution)/shard_map/ppermute | solution.py:65
  14.5 4.4 %collective-permute-start.3 = (bf16[128,16,256]{2,1,0:T(8,128)(2,1)S(1)}, bf16[128,16,256]{2,1,0:T(8,128)(2,1)S(1)}, u32[]{:S(2)}, u32[]{:S(2)}) collective-permute-start(bf16[128,16,256]{2,1,0:T(8,128)(2,1)S(1)} %get-tuple-element.55), channel_id=1, source_target_pairs={{0,1},{1,0},{2,3},{3,2},{4,5},{5,4},{6,7},{7,6},{8,9},{9,8},{10,11... | collective-permute-start | bytes 3145736 | tf_op jit(solution)/shard_map/ppermute | solution.py:65
  14.6 4.3 %collective-permute-start.1 = (bf16[2,16,512]{2,1,0:T(8,128)(2,1)S(1)}, bf16[2,16,512]{2,1,0:T(8,128)(2,1)S(1)}, u32[]{:S(2)}, u32[]{:S(2)}) collective-permute-start(bf16[2,16,512]{2,1,0:T(8,128)(2,1)S(1)} %pad_maximum_fusion.11), channel_id=1, source_target_pairs={{0,8},{1,9},{2,10},{3,11},{4,12},{5,13},{6,14},{7,15},{8,0},{9,1},... | collective-permute-start | bytes 98312 | tf_op jit(solution)/shard_map/ppermute | solution.py:65
  19.1 23.9 %copy-start.4 = (s32[2048]{0:T(1024)S(1)}, s32[2048]{0:T(1024)}, u32[]{:S(2)}) copy-start(s32[2048]{0:T(1024)} %constant.45.clone.table_hbm.table_ref) | copy-start | bytes 24580
  19.3 14.9 %collective-permute-start.6 = (bf16[64,16,256]{2,1,0:T(8,128)(2,1)S(1)}, bf16[64,16,256]{2,1,0:T(8,128)(2,1)S(1)}, u32[]{:S(2)}, u32[]{:S(2)}) collective-permute-start(bf16[64,16,256]{2,1,0:T(8,128)(2,1)S(1)} %get-tuple-element.64), channel_id=1, source_target_pairs={{0,2},{1,33},{2,0},{3,35},{4,6},{5,37},{6,4},{7,39},{8,10},{9,41},... | collective-permute-start | bytes 1572872 | tf_op jit(solution)/shard_map/ppermute | solution.py:65
  21.5 12.8 %collective-permute-start.7 = (bf16[64,16,256]{2,1,0:T(8,128)(2,1)S(1)}, bf16[64,16,256]{2,1,0:T(8,128)(2,1)S(1)}, u32[]{:S(2)}, u32[]{:S(2)}) collective-permute-start(bf16[64,16,256]{2,1,0:T(8,128)(2,1)S(1)} %get-tuple-element.65), channel_id=1, source_target_pairs={{0,6},{1,97},{2,4},{3,99},{4,2},{5,101},{6,0},{7,103},{8,14},{9,10... | collective-permute-start | bytes 1572872 | tf_op jit(solution)/shard_map/ppermute | solution.py:65
  23.4 5.5 %collective-permute-start.4 = (bf16[4,16,512]{2,1,0:T(8,128)(2,1)S(1)}, bf16[4,16,512]{2,1,0:T(8,128)(2,1)S(1)}, u32[]{:S(2)}, u32[]{:S(2)}) collective-permute-start(bf16[4,16,512]{2,1,0:T(8,128)(2,1)S(1)} %pad_maximum_fusion.9), channel_id=1, source_target_pairs={{0,24},{1,25},{2,26},{3,27},{4,28},{5,29},{6,30},{7,31},{8,16},{9,... | collective-permute-start | bytes 196616 | tf_op jit(solution)/shard_map/ppermute | solution.py:65
  28.9 5.4 %collective-permute-start.5 = (bf16[8,16,512]{2,1,0:T(8,128)(2,1)S(1)}, bf16[8,16,512]{2,1,0:T(8,128)(2,1)S(1)}, u32[]{:S(2)}, u32[]{:S(2)}) collective-permute-start(bf16[8,16,512]{2,1,0:T(8,128)(2,1)S(1)} %pad_maximum_fusion.6), channel_id=1, source_target_pairs={{0,96},{1,7},{2,98},{3,5},{4,100},{5,3},{6,102},{7,1},{8,104},{9,1... | collective-permute-start | bytes 393224 | tf_op jit(solution)/shard_map/ppermute | solution.py:65
  34.5 5.3 %collective-permute-start.10 = (bf16[16,16,512]{2,1,0:T(8,128)(2,1)S(1)}, bf16[16,16,512]{2,1,0:T(8,128)(2,1)S(1)}, u32[]{:S(2)}, u32[]{:S(2)}) collective-permute-start(bf16[16,16,512]{2,1,0:T(8,128)(2,1)S(1)} %pad_maximum_fusion.4), channel_id=1, source_target_pairs={{0,32},{1,3},{2,34},{3,1},{4,36},{5,7},{6,38},{7,5},{8,40},{9,11},... | collective-permute-start | bytes 786440 | tf_op jit(solution)/shard_map/ppermute | solution.py:65
  35.5 6.4 %collective-permute-start.8 = (bf16[32,16,256]{2,1,0:T(8,128)(2,1)S(1)}, bf16[32,16,256]{2,1,0:T(8,128)(2,1)S(1)}, u32[]{:S(2)}, u32[]{:S(2)}) collective-permute-start(bf16[32,16,256]{2,1,0:T(8,128)(2,1)S(1)} %get-tuple-element.73), channel_id=1, source_target_pairs={{0,6},{1,97},{2,4},{3,99},{4,2},{5,101},{6,0},{7,103},{8,14},{9,10... | collective-permute-start | bytes 786440 | tf_op jit(solution)/shard_map/ppermute | solution.py:65
  36.7 6.3 %collective-permute-start.9 = (bf16[32,16,256]{2,1,0:T(8,128)(2,1)S(1)}, bf16[32,16,256]{2,1,0:T(8,128)(2,1)S(1)}, u32[]{:S(2)}, u32[]{:S(2)}) collective-permute-start(bf16[32,16,256]{2,1,0:T(8,128)(2,1)S(1)} %get-tuple-element.75), channel_id=1, source_target_pairs={{0,2},{1,33},{2,0},{3,35},{4,6},{5,37},{6,4},{7,39},{8,10},{9,41},... | collective-permute-start | bytes 786440 | tf_op jit(solution)/shard_map/ppermute | solution.py:65
  44.0 4.5 %collective-permute-start.14 = (f32[16,128]{1,0:T(8,128)S(1)}, f32[16,128]{1,0:T(8,128)S(1)}, u32[]{:S(2)}, u32[]{:S(2)}) collective-permute-start(f32[16,128]{1,0:T(8,128)S(1)} %get-tuple-element.79), channel_id=1, source_target_pairs={{0,4},{1,65},{2,6},{3,67},{4,0},{5,69},{6,2},{7,71},{8,12},{9,73},... | collective-permute-start | bytes 24584 | tf_op jit(solution)/shard_map/ppermute | solution.py:65
  44.2 6.6 %collective-permute-start.13 = (f32[16,128]{1,0:T(8,128)S(1)}, f32[16,128]{1,0:T(8,128)S(1)}, u32[]{:S(2)}, u32[]{:S(2)}) collective-permute-start(f32[16,128]{1,0:T(8,128)S(1)} %get-tuple-element.79), channel_id=1, source_target_pairs={{0,6},{1,97},{2,4},{3,99},{4,2},{5,101},{6,0},{7,103},{8,14},{9,10... | collective-permute-start | bytes 24584 | tf_op jit(solution)/shard_map/ppermute | solution.py:65
  46.4 4.4 %collective-permute-start.12 = (f32[16,128]{1,0:T(8,128)S(1)}, f32[16,128]{1,0:T(8,128)S(1)}, u32[]{:S(2)}, u32[]{:S(2)}) collective-permute-start(f32[16,128]{1,0:T(8,128)S(1)} %get-tuple-element.79), channel_id=1, source_target_pairs={{0,2},{1,33},{2,0},{3,35},{4,6},{5,37},{6,4},{7,39},{8,10},{9,41},... | collective-permute-start | bytes 24584 | tf_op jit(solution)/shard_map/ppermute | solution.py:65
  46.8 9.0 %collective-permute-start.22 = (bf16[32,16,256]{2,1,0:T(8,128)(2,1)S(1)}, bf16[32,16,256]{2,1,0:T(8,128)(2,1)S(1)}, u32[]{:S(2)}, u32[]{:S(2)}) collective-permute-start(bf16[32,16,256]{2,1,0:T(8,128)(2,1)S(1)} %get-tuple-element.101), channel_id=1, source_target_pairs={{0,2},{1,33},{2,0},{3,35},{4,6},{5,37},{6,4},{7,39},{8,10},{9,41},... | collective-permute-start | bytes 786440 | tf_op jit(solution)/shard_map/ppermute | solution.py:65
  48.0 8.3 %collective-permute-start.19 = (bf16[32,16,256]{2,1,0:T(8,128)(2,1)S(1)}, bf16[32,16,256]{2,1,0:T(8,128)(2,1)S(1)}, u32[]{:S(2)}, u32[]{:S(2)}) collective-permute-start(bf16[32,16,256]{2,1,0:T(8,128)(2,1)S(1)} %get-tuple-element.102), channel_id=1, source_target_pairs={{0,6},{1,97},{2,4},{3,99},{4,2},{5,101},{6,0},{7,103},{8,14},{9,10... | collective-permute-start | bytes 786440 | tf_op jit(solution)/shard_map/ppermute | solution.py:65
  48.4 8.0 %collective-permute-start.11 = (bf16[16,16,512]{2,1,0:T(8,128)(2,1)S(1)}, bf16[16,16,512]{2,1,0:T(8,128)(2,1)S(1)}, u32[]{:S(2)}, u32[]{:S(2)}) collective-permute-start(bf16[16,16,512]{2,1,0:T(8,128)(2,1)S(1)} %get-tuple-element.78), channel_id=1, source_target_pairs={{0,32},{1,3},{2,34},{3,1},{4,36},{5,7},{6,38},{7,5},{8,40},{9,11},... | collective-permute-start | bytes 786440 | tf_op jit(solution)/shard_map/ppermute | solution.py:65
  50.8 21.3 %collective-permute-start.16 = (f32[16,128]{1,0:T(8,128)S(1)}, f32[16,128]{1,0:T(8,128)S(1)}, u32[]{:S(2)}, u32[]{:S(2)}) collective-permute-start(f32[16,128]{1,0:T(8,128)S(1)} %get-tuple-element.100), channel_id=1, source_target_pairs={{0,32},{1,3},{2,34},{3,1},{4,36},{5,7},{6,38},{7,5},{8,40},{9,11},... | collective-permute-start | bytes 24584 | tf_op jit(solution)/shard_map/ppermute | solution.py:65
  51.4 20.7 %collective-permute-start.17 = (f32[16,128]{1,0:T(8,128)S(1)}, f32[16,128]{1,0:T(8,128)S(1)}, u32[]{:S(2)}, u32[]{:S(2)}) collective-permute-start(f32[16,128]{1,0:T(8,128)S(1)} %get-tuple-element.100), channel_id=1, source_target_pairs={{0,64},{1,5},{2,66},{3,7},{4,68},{5,1},{6,70},{7,3},{8,72},{9,13},... | collective-permute-start | bytes 24584 | tf_op jit(solution)/shard_map/ppermute | solution.py:65
  55.8 15.9 %collective-permute-start.23 = (bf16[64,16,256]{2,1,0:T(8,128)(2,1)S(1)}, bf16[64,16,256]{2,1,0:T(8,128)(2,1)S(1)}, u32[]{:S(2)}, u32[]{:S(2)}) collective-permute-start(bf16[64,16,256]{2,1,0:T(8,128)(2,1)S(1)} %pad_maximum_fusion.3), channel_id=1, source_target_pairs={{0,6},{1,97},{2,4},{3,99},{4,2},{5,101},{6,0},{7,103},{8,14},{9,10... | collective-permute-start | bytes 1572872 | tf_op jit(solution)/shard_map/ppermute | solution.py:65
  56.4 10.4 %collective-permute-start.20 = (bf16[64,16,256]{2,1,0:T(8,128)(2,1)S(1)}, bf16[64,16,256]{2,1,0:T(8,128)(2,1)S(1)}, u32[]{:S(2)}, u32[]{:S(2)}) collective-permute-start(bf16[64,16,256]{2,1,0:T(8,128)(2,1)S(1)} %pad_maximum_fusion.2), channel_id=1, source_target_pairs={{0,2},{1,33},{2,0},{3,35},{4,6},{5,37},{6,4},{7,39},{8,10},{9,41},... | collective-permute-start | bytes 1572872 | tf_op jit(solution)/shard_map/ppermute | solution.py:65
  56.6 15.4 %collective-permute-start.15 = (bf16[9,16,512]{2,1,0:T(8,128)(2,1)S(1)}, bf16[9,16,512]{2,1,0:T(8,128)(2,1)S(1)}, u32[]{:S(2)}, u32[]{:S(2)}) collective-permute-start(bf16[9,16,512]{2,1,0:T(8,128)(2,1)S(1)} %pad_maximum_fusion.5), channel_id=1, source_target_pairs={{0,96},{1,7},{2,98},{3,5},{4,100},{5,3},{6,102},{7,1},{8,104},{9,1... | collective-permute-start | bytes 442376 | tf_op jit(solution)/shard_map/ppermute | solution.py:65
  66.8 10.6 %collective-permute-start.21 = (bf16[128,16,256]{2,1,0:T(8,128)(2,1)S(1)}, bf16[128,16,256]{2,1,0:T(8,128)(2,1)S(1)}, u32[]{:S(2)}, u32[]{:S(2)}) collective-permute-start(bf16[128,16,256]{2,1,0:T(8,128)(2,1)S(1)} %pad_maximum_fusion.own0_ref), channel_id=1, source_target_pairs={{0,1},{1,0},{2,3},{3,2},{4,5},{5,4},{6,7},{7,6},{8,9},{9,8},{10,11... | collective-permute-start | bytes 3145736 | tf_op jit(solution)/shard_map/ppermute | solution.py:65
  71.9 5.6 %collective-permute-start.24 = (bf16[128,16,256]{2,1,0:T(8,128)(2,1)S(1)}, bf16[128,16,256]{2,1,0:T(8,128)(2,1)S(1)}, u32[]{:S(2)}, u32[]{:S(2)}) collective-permute-start(bf16[128,16,256]{2,1,0:T(8,128)(2,1)S(1)} %pad_maximum_fusion.1.own1_ref), channel_id=1, source_target_pairs={{0,1},{1,0},{2,3},{3,2},{4,5},{5,4},{6,7},{7,6},{8,9},{9,8},{10,11... | collective-permute-start | bytes 3145736 | tf_op jit(solution)/shard_map/ppermute | solution.py:65
  72.1 12.0 %collective-permute-start.25 = (f32[16,128]{1,0:T(8,128)S(1)}, f32[16,128]{1,0:T(8,128)S(1)}, u32[]{:S(2)}, u32[]{:S(2)}) collective-permute-start(f32[16,128]{1,0:T(8,128)S(1)} %get-tuple-element.98), channel_id=1, source_target_pairs={{0,1},{1,0},{2,3},{3,2},{4,5},{5,4},{6,7},{7,6},{8,9},{9,8},{10,11... | collective-permute-start | bytes 24584 | tf_op jit(solution)/shard_map/ppermute | solution.py:65
  72.6 11.5 %collective-permute-start.26 = (f32[16,128]{1,0:T(8,128)S(1)}, f32[16,128]{1,0:T(8,128)S(1)}, u32[]{:S(2)}, u32[]{:S(2)}) collective-permute-start(f32[16,128]{1,0:T(8,128)S(1)} %get-tuple-element.98), channel_id=1, source_target_pairs={{0,25},{1,24},{2,27},{3,26},{4,29},{5,28},{6,31},{7,30},{8,17},{9,... | collective-permute-start | bytes 24584 | tf_op jit(solution)/shard_map/ppermute | solution.py:65
  77.1 6.9 %collective-permute-start.18 = (bf16[5,16,512]{2,1,0:T(8,128)(2,1)S(1)}, bf16[5,16,512]{2,1,0:T(8,128)(2,1)S(1)}, u32[]{:S(2)}, u32[]{:S(2)}) collective-permute-start(bf16[5,16,512]{2,1,0:T(8,128)(2,1)S(1)} %pad_maximum_fusion.8), channel_id=1, source_target_pairs={{0,24},{1,25},{2,26},{3,27},{4,28},{5,29},{6,30},{7,31},{8,16},{9,... | collective-permute-start | bytes 245768 | tf_op jit(solution)/shard_map/ppermute | solution.py:65
  84.1 11.9 %copy-start.7 = (f32[16,512]{1,0:T(8,128)S(1)}, f32[16,512]{1,0:T(8,128)}, u32[]{:S(2)}) copy-start(f32[16,512]{1,0:T(8,128)} %param.10) | copy-start | bytes 98308
  84.2 11.9 %copy-start.8 = (f32[16,512]{1,0:T(8,128)S(1)}, f32[16,512]{1,0:T(8,128)}, u32[]{:S(2)}) copy-start(f32[16,512]{1,0:T(8,128)} %param.11) | copy-start | bytes 98308
  84.2 7.7 %collective-permute-start.27 = (f32[3,16,512]{2,1,0:T(8,128)S(1)}, f32[3,16,512]{2,1,0:T(8,128)S(1)}, u32[]{:S(2)}, u32[]{:S(2)}) collective-permute-start(f32[3,16,512]{2,1,0:T(8,128)S(1)} %pad_maximum_fusion.7), channel_id=1, source_target_pairs={{0,8},{1,9},{2,10},{3,11},{4,12},{5,13},{6,14},{7,15},{8,0},{9,1},... | collective-permute-start | bytes 294920 | tf_op jit(solution)/shard_map/ppermute | solution.py:65
  92.0 3.2 %collective-permute-start.28 = (f32[2,16,512]{2,1,0:T(8,128)S(1)}, f32[2,16,512]{2,1,0:T(8,128)S(1)}, u32[]{:S(2)}, u32[]{:S(2)}) collective-permute-start(f32[2,16,512]{2,1,0:T(8,128)S(1)} %pad_maximum_fusion.10), channel_id=1, source_target_pairs={{0,128},{1,129},{2,130},{3,131},{4,132},{5,133},{6,134},{7,135},{8... | collective-permute-start | bytes 196616 | tf_op jit(solution)/shard_map/ppermute | solution.py:65
  (7 other events, 19.4 us)
